TPU v7x, 32 devices: a whole 2x2x4 slice. The times are simulated.
32 devices in a mesh: dp: 4 (over x, core), seq: 8 (over z, y).
Axes of the slice: x: 2, y: 2, z: 4, core: 2. Of those that a mesh axis runs over, the one named last changes fastest.
Arguments:
- tokens: bfloat16 [24, 3072, 512], P('dp', 'seq'), may hold values from -6 to 6
- short_counts: int32 [4], P('dp'), may hold values from 1 to 5, as said below
- norm1_gain: bfloat16 [512], replicated, may hold values from 0.5 to 1.5
- norm1_bias: bfloat16 [512], replicated, may hold values from -1.25 to 1.25
- query_weight: bfloat16 [512, 512], replicated, may hold values from -0.25 to 0.25
- query_bias: bfloat16 [512], replicated, may hold values from -1.25 to 1.25
- key_weight: bfloat16 [512, 512], replicated, may hold values from -0.25 to 0.25
- key_bias: bfloat16 [512], replicated, may hold values from -1.25 to 1.25
- value_weight: bfloat16 [512, 512], replicated, may hold values from -0.25 to 0.25
- value_bias: bfloat16 [512], replicated, may hold values from -1.25 to 1.25
- output_weight: bfloat16 [512, 512], replicated, may hold values from -1.5 to 1.5
- output_bias: bfloat16 [512], replicated, may hold values from -1.25 to 1.25
- norm2_gain: bfloat16 [512], replicated, may hold values from 0.5 to 1.5
- norm2_bias: bfloat16 [512], replicated, may hold values from -1.25 to 1.25
- hidden_weight: bfloat16 [512, 2048], replicated, may hold values from -0.25 to 0.25
- hidden_bias: bfloat16 [2048], replicated, may hold values from -1.25 to 1.25
- return_weight: bfloat16 [2048, 512], replicated, may hold values from -0.125 to 0.125
- return_bias: bfloat16 [512], replicated, may hold values from -1.25 to 1.25
- cotangent: bfloat16 [24, 3072, 512], P('dp', 'seq'), may hold values from -6 to 6
Outputs:
- layer_out: bfloat16 [24, 3072, 512], P('dp', 'seq')
- input_grad: bfloat16 [24, 3072, 512], P('dp', 'seq')
- den_peak: float32 [], replicated
- grad_norm1_gain: float32 [512], replicated
- grad_norm1_bias: float32 [512], replicated
- grad_query_weight: float32 [512, 512], replicated
- grad_query_bias: float32 [512], replicated
- grad_key_weight: float32 [512, 512], replicated
- grad_key_bias: float32 [512], replicated
- grad_value_weight: float32 [512, 512], replicated
- grad_value_bias: float32 [512], replicated
- grad_output_weight: float32 [512, 512], replicated
- grad_output_bias: float32 [512], replicated
- grad_norm2_gain: float32 [512], replicated
- grad_norm2_bias: float32 [512], replicated
- grad_hidden_weight: float32 [512, 2048], replicated
- grad_hidden_bias: float32 [2048], replicated
- grad_return_weight: float32 [2048, 512], replicated
- grad_return_bias: float32 [512], replicated
Inputs may be any that keep to these rules, and one draw needn't show every extreme that they name: `short_counts`: each dp index has at least one image of each resolution; every draw has an index with a single short image and one with 5.
All inputs are finite; a program needn't handle non-finite values.
Results may differ from a plain program's by a relative error of at most 0.012.
Values sent between devices are 32-bit elements; how exact they have to be, the bound alone decides.
A program may use at most 320 MiB of HBM per device.

v0:
```python
from functools import partial

import jax
import jax.numpy as jnp
from jax import lax
from jax.sharding import PartitionSpec as P

HEADS = 8
LEN_LONG = 3072
LEN_SHORT = 784


EPSILON = 1e-05
HIGH = lax.Precision.HIGHEST


def entering(part, axis, combine, identity, reverse):
    count = lax.axis_size(axis)
    place = lax.axis_index(axis)
    ahead = count - 1 - place if reverse else place
    gathered = jax.tree.map(lambda a: lax.all_gather(a, axis), part)
    state = jax.tree.map(lambda a, e: jnp.zeros_like(a) + jnp.asarray(e, a.dtype), part, identity)

    def one(hop, state):
        source = count - 1 - hop if reverse else hop
        return combine(
            state, jax.tree.map(lambda a: lax.dynamic_index_in_dim(a, source, 0, False), gathered)
        )

    return lax.fori_loop(0, ahead, one, state)


def layer_norm(values, gain, shift):
    centre = values - jnp.mean(values, axis=-1, keepdims=True)
    spread = jnp.mean(centre * centre, axis=-1, keepdims=True)
    return centre * lax.rsqrt(spread + EPSILON) * gain + shift


def feature(values):
    return jnp.where(values > 0, values + 1.0, jnp.exp(jnp.minimum(values, 0.0)))


def feature_slope(values):
    return jnp.where(values > 0, 1.0, jnp.exp(jnp.minimum(values, 0.0)))


def matmul(left, right):
    return jnp.dot(left, right, preferred_element_type=jnp.float32)


def inner_rows(left, right):
    return lax.dot_general(
        left, right, (((0,), (0,)), ((), ())), preferred_element_type=jnp.float32
    )


def times_transposed(left, right):
    return lax.dot_general(
        left, right, (((1,), (1,)), ((), ())), preferred_element_type=jnp.float32
    )


def add_pair(earlier, later):
    return (earlier[0] + later[0], earlier[1] + later[1])


def column_sum(values):
    return jnp.sum(values.astype(jnp.float32), axis=0)


def per_device(
    tokens,
    short_counts,
    norm1_gain,
    norm1_bias,
    query_weight,
    query_bias,
    key_weight,
    key_bias,
    value_weight,
    value_bias,
    output_weight,
    output_bias,
    norm2_gain,
    norm2_bias,
    hidden_weight,
    hidden_bias,
    return_weight,
    return_bias,
    cotangent,
):
    images, span, width = tokens.shape
    depth = width // HEADS
    flat = images * span
    four = (images, span, HEADS, depth)
    stream = tokens.astype(jnp.float32).reshape(flat, width)
    seq_index = lax.axis_index("seq")
    total_length = span * lax.axis_size("seq")
    position = seq_index * span + jnp.arange(span, dtype=jnp.int32)
    image_ids = jnp.arange(images, dtype=jnp.int32)
    limits = jnp.where(image_ids < short_counts[0], LEN_SHORT, LEN_LONG)
    valid = (position[None, :] < limits[:, None]).astype(jnp.float32)
    normed_one, norm_one_pull = jax.vjp(
        layer_norm, stream, norm1_gain.astype(jnp.float32), norm1_bias.astype(jnp.float32)
    )
    first_in = normed_one.astype(jnp.bfloat16)
    query_pre = matmul(first_in, query_weight) + query_bias.astype(jnp.float32)
    key_pre = matmul(first_in, key_weight) + key_bias.astype(jnp.float32)
    value_pre = matmul(first_in, value_weight) + value_bias.astype(jnp.float32)
    query_low = feature(query_pre).astype(jnp.bfloat16)
    key_low = (feature(key_pre).reshape(images, span, width) * valid[:, :, None]).astype(
        jnp.bfloat16
    )
    value_low = value_pre.astype(jnp.bfloat16)
    query_half = query_low.reshape(four)
    key_half = key_low.reshape(four)
    value_half = value_low.reshape(four)
    query_four = query_half.astype(jnp.float32)
    key_four = key_half.astype(jnp.float32)
    value_four = value_half.astype(jnp.float32)
    own_state = jnp.einsum(
        "rshd,rshe->rhde", key_half, value_half, preferred_element_type=jnp.float32
    )
    own_sum = jnp.sum(key_four, axis=1)
    empty_state = jnp.zeros_like(own_state)
    empty_sum = jnp.zeros_like(own_sum)
    prior_state, prior_sum = entering(
        (own_state, own_sum), "seq", add_pair, (empty_state, empty_sum), False
    )
    lower = jnp.tril(jnp.ones((span, span), jnp.float32))
    scores = (
        jnp.einsum("rthd,rshd->rhts", query_half, key_half, preferred_element_type=jnp.float32)
        * lower
    )
    numer = jnp.einsum("rhts,rshe->rthe", scores, value_four, precision=HIGH)
    numer = numer + jnp.einsum("rthd,rhde->rthe", query_four, prior_state, precision=HIGH)
    denom = jnp.transpose(jnp.sum(scores, axis=3), (0, 2, 1))
    denom = denom + jnp.einsum("rthd,rhd->rth", query_four, prior_sum, precision=HIGH)
    mixed = numer / denom[..., None]
    local_peak = jnp.max(jnp.where(valid[:, :, None] > 0, denom, 0.0)) / (total_length * depth)
    den_peak = lax.pmax(local_peak, ("dp", "seq"))
    attn = mixed.reshape(flat, width).astype(jnp.bfloat16)
    middle = stream + matmul(attn, output_weight) + output_bias.astype(jnp.float32)
    normed_two, norm_two_pull = jax.vjp(
        layer_norm, middle, norm2_gain.astype(jnp.float32), norm2_bias.astype(jnp.float32)
    )
    second_in = normed_two.astype(jnp.bfloat16)
    hidden_pre = matmul(second_in, hidden_weight) + hidden_bias.astype(jnp.float32)
    hidden_act, gelu_pull = jax.vjp(partial(jax.nn.gelu, approximate=False), hidden_pre)
    act_low = hidden_act.astype(jnp.bfloat16)
    result = middle + matmul(act_low, return_weight) + return_bias.astype(jnp.float32)
    layer_out = result.astype(jnp.bfloat16).reshape(images, span, width)
    upstream = cotangent.reshape(flat, width)
    grad_return_weight = inner_rows(act_low, upstream)
    grad_return_bias = column_sum(upstream)
    (pre_grad,) = gelu_pull(times_transposed(upstream, return_weight))
    pre_low = pre_grad.astype(jnp.bfloat16)
    grad_hidden_weight = inner_rows(second_in, pre_low)
    grad_hidden_bias = column_sum(pre_low)
    norm_two_back, grad_norm2_gain, grad_norm2_bias = norm_two_pull(
        times_transposed(pre_low, hidden_weight)
    )
    residual_grad = upstream.astype(jnp.float32) + norm_two_back
    ffn_grads = (
        grad_norm2_gain,
        grad_norm2_bias,
        grad_hidden_weight,
        grad_hidden_bias,
        grad_return_weight,
        grad_return_bias,
    )
    mid_low = residual_grad.astype(jnp.bfloat16)
    grad_output_weight = inner_rows(attn, mid_low)
    grad_output_bias = column_sum(mid_low)
    mixed_grad = times_transposed(mid_low, output_weight).reshape(four)
    inverse = 1.0 / denom
    numer_grad = mixed_grad * inverse[..., None]
    denom_grad = -jnp.sum(mixed_grad * mixed, axis=-1) * inverse
    own_grad = jnp.einsum("rthd,rthe->rhde", query_four, numer_grad, precision=HIGH)
    own_gsum = jnp.einsum("rth,rthd->rhd", denom_grad, query_four, precision=HIGH)
    later_state, later_sum = entering(
        (own_grad, own_gsum), "seq", add_pair, (empty_state, empty_sum), True
    )
    weights_back = jnp.einsum("rthe,rshe->rhts", numer_grad, value_four, precision=HIGH)
    weights_back = (weights_back + jnp.transpose(denom_grad, (0, 2, 1))[..., None]) * lower
    query_side = jnp.einsum("rhts,rshd->rthd", weights_back, key_four, precision=HIGH)
    query_side = query_side + jnp.einsum("rhde,rthe->rthd", prior_state, numer_grad, precision=HIGH)
    query_side = query_side + prior_sum[:, None] * denom_grad[..., None]
    key_side = jnp.einsum("rhts,rthd->rshd", weights_back, query_four, precision=HIGH)
    key_side = key_side + jnp.einsum("rhde,rshe->rshd", later_state, value_four, precision=HIGH)
    key_side = key_side + later_sum[:, None]
    value_side = jnp.einsum("rhts,rthe->rshe", scores, numer_grad, precision=HIGH)
    value_side = value_side + jnp.einsum("rshd,rhde->rshe", key_four, later_state, precision=HIGH)
    query_grad = (query_side.reshape(flat, width) * feature_slope(query_pre)).astype(jnp.bfloat16)
    key_masked = (key_side.reshape(images, span, width) * valid[:, :, None]).reshape(flat, width)
    key_grad = (key_masked * feature_slope(key_pre)).astype(jnp.bfloat16)
    value_grad = value_side.reshape(flat, width).astype(jnp.bfloat16)
    grad_query_weight = inner_rows(first_in, query_grad)
    grad_key_weight = inner_rows(first_in, key_grad)
    grad_value_weight = inner_rows(first_in, value_grad)
    first_grad = times_transposed(query_grad, query_weight) + times_transposed(key_grad, key_weight)
    first_grad = first_grad + times_transposed(value_grad, value_weight)
    norm_one_back, grad_norm1_gain, grad_norm1_bias = norm_one_pull(first_grad)
    input_grad = (residual_grad + norm_one_back).astype(jnp.bfloat16).reshape(images, span, width)
    attn_grads = (
        grad_norm1_gain,
        grad_norm1_bias,
        grad_query_weight,
        column_sum(query_grad),
        grad_key_weight,
        column_sum(key_grad),
        grad_value_weight,
        column_sum(value_grad),
        grad_output_weight,
        grad_output_bias,
    )
    summed = lax.psum(attn_grads + ffn_grads, ("dp", "seq"))
    attn_grads = summed[:10]
    ffn_grads = summed[10:]
    return (
        layer_out,
        input_grad,
        den_peak,
        attn_grads[0],
        attn_grads[1],
        attn_grads[2],
        attn_grads[3],
        attn_grads[4],
        attn_grads[5],
        attn_grads[6],
        attn_grads[7],
        attn_grads[8],
        attn_grads[9],
        ffn_grads[0],
        ffn_grads[1],
        ffn_grads[2],
        ffn_grads[3],
        ffn_grads[4],
        ffn_grads[5],
    )


def solution(mesh):
    return jax.shard_map(
        per_device,
        mesh=mesh,
        in_specs=(
            P("dp", "seq", None),
            P("dp"),
            P(),
            P(),
            P(),
            P(),
            P(),
            P(),
            P(),
            P(),
            P(),
            P(),
            P(),
            P(),
            P(),
            P(),
            P(),
            P(),
            P("dp", "seq", None),
        ),
        out_specs=(
            P("dp", "seq", None),
            P("dp", "seq", None),
            P(),
            P(),
            P(),
            P(),
            P(),
            P(),
            P(),
            P(),
            P(),
            P(),
            P(),
            P(),
            P(),
            P(),
            P(),
            P(),
            P(),
        ),
        check_vma=False,
    )
```

profile of v0, /device:TPU:0, one launch (start us, length us, event | category | flops | bytes accessed | tf_op | source)
XLA Modules:
  0.0 905.8 jit_solution(10727979827520118298)
XLA Ops:
  14.9 5.6 add_select_fusion
  20.6 7.9 reshape.288
  28.5 8.2 copy.130
  37.4 4.5 fusion.21
  41.9 7.1 reshape.291
  48.9 6.4 copy.132
  62.1 6.6 select_convert_fusion
  68.7 7.1 reshape.292
  75.8 6.5 copy.131
  83.6 33.8 %all-gather.1 = f32[48,8,64]{2,1,0:T(8,128)S(1)} all-gather(f32[6,8,64]{2,1,0:T(8,128)S(1)} %get-tuple-element.197), channel_id=3, replica_groups=mesh['dp'=4,'seq'=8] {'seq'}, dimensions={0}, use_global_device_ids=true | all-gather | bytes 110592 | tf_op jit(solution)/shard_map/all_gather | solution.py:21
  121.0 11.4 %multiply_reduce_fusion = (f32[6,8,384]{2,1,0:T(8,128)S(1)}, f32[6,8,384,384]{2,3,1,0:T(8,128)}) fusion(f32[384,384]{0,1:T(8,128)S(1)} %fusion.35, bf16[6,384,8,64]{1,3,2,0:T(8,128)(2,1)S(1)} %copy-done.4, bf16[6,384,8,64]{1,3,2,0:T(8,128)(2,1)S(1)} %copy-done.7), kind=kOutput, calls=%fused_computation.10 | convolution fusion | flops 920107008 | bytes 33693696 | tf_op jit(solution)/shard_map/rthd,rshd->rhts/dot_general | solution.py:132
  132.4 17.3 %fusion.4 = f32[6,8,64,384]{3,2,1,0:T(8,128)} fusion(bf16[6,384,8,64]{1,3,2,0:T(8,128)(2,1)} %copy.132, f32[6,8,384,384]{2,3,1,0:T(8,128)} %get-tuple-element.210, f32[384,384]{0,1:T(8,128)S(1)} %fusion.35), kind=kOutput, calls=%fused_computation.11 | convolution fusion | flops 5442895872 | bytes 35979264 | tf_op jit(solution)/shard_map/rhts,rshe->rthe/dot_general | solution.py:135
  149.7 93.2 %all-gather.7.cloned.1.call-done = f32[48,8,64,64]{3,2,1,0:T(8,128)} async-done(((f32[6,8,64,64]{3,2,1,0:T(8,128)}), f32[48,8,64,64]{3,2,1,0:T(8,128)}) %all-gather.7.cloned.1.call-update) | async-done | bytes 6291472 | tf_op jit(solution)/shard_map/all_gather | solution.py:21
  247.9 8.1 fusion.53
  260.9 49.0 %multiply_convert_fusion = (bf16[2304,2048]{1,0:T(8,128)(2,1)}, f32[2304,2048]{1,0:T(8,128)}, f32[2304,2048]{1,0:T(8,128)}) fusion(f32[2048]{0:T(1024)S(1)} %convert_element_type.152, bf16[512,2048]{1,0:T(8,128)(2,1)S(1)} %copy-done, f32[2304,512]{1,0:T(8,128)S(1)} %get-tuple-element.214, f32[512]{0:T(512)S(1)} %convert_element_type.150, ...), kind=kOutput, calls=%fused_computation.16 | convolution fusion | flops 5149163520 | bytes 54032384 | tf_op jit(solution)/shard_map/dot_general | solution.py:48
  309.9 21.8 %convert_reduce_fusion = (f32[2048]{0:T(1024)}, bf16[2304,2048]{1,0:T(8,128)(2,1)}) fusion(f32[2304,2048]{1,0:T(8,128)} %get-tuple-element.196, bf16[2304,512]{1,0:T(8,128)(2,1)S(1)} %bitcast.152, bf16[2048,512]{1,0:T(8,128)(2,1)} %param.39, f32[2304,2048]{1,0:T(8,128)} %get-tuple-element.215, f32[2048]{0:T(1024)S(1)} %convert_element_type.152), kind=kOutput, calls=%fused_computation.14 | convolution fusion | flops 4912052224 | bytes 51658752 | tf_op jit(solution)/shard_map/dot_general | solution.py:58
  331.7 10.3 %multiply_reduce_fusion.1 = (f32[512]{0:T(512)}, f32[2304]{0:T(1024)S(1)}, f32[512]{0:T(512)}, f32[2304,512]{1,0:T(8,128)S(1)}) fusion(f32[2304,512]{1,0:T(8,128)S(1)} %get-tuple-element.214, f32[2304]{0:T(1024)S(1)} %fusion.43, f32[2304]{0:T(1024)S(1)} %broadcast_multiply_fusion, f32[512]{0:T(512)S(1)} %convert_element_type.149, ...), kind=kOutput, calls=%fused_computation.52 | convolution fusion | flops 4841271808 | bytes 21005312 | tf_op jit(solution)/shard_map/dot_general | solution.py:58
  348.1 3.7 fusion.57
  351.8 6.5 reshape.276
  358.3 5.7 multiply_reduce_fusion.4
  365.1 4.6 fusion.23
  369.8 9.2 %fusion.25 = f32[6,8,384,64]{2,3,1,0:T(8,128)} fusion(f32[6,8,64,64]{3,2,1,0:T(8,128)S(1)} %copy-done.9, f32[6,384,8]{1,2,0:T(8,128)S(1)} %get-tuple-element.200, f32[6,384,8,64]{1,0,3,2:T(8,128)} %reshape.276), kind=kOutput, calls=%fused_computation.83 | convolution fusion | flops 907149312 | bytes 10297344 | tf_op jit(solution)/shard_map/rhde,rthe->rthd/dot_general | solution.py:187
  379.0 18.5 %fusion.27 = f32[6,8,384,384]{2,3,1,0:T(8,128)} fusion(bf16[6,384,8,64]{1,3,2,0:T(8,128)(2,1)S(1)} %copy-done.11, f32[6,384,8]{1,2,0:T(8,128)S(1)} %get-tuple-element.200, f32[6,384,8,64]{1,0,3,2:T(8,128)} %reshape.276), kind=kOutput, calls=%fused_computation.85 | convolution fusion | flops 5436997632 | bytes 35463168 | tf_op jit(solution)/shard_map/rthe,rshe->rhts/dot_general | solution.py:184
  397.5 19.4 %fusion.20 = f32[6,384,8,64]{1,3,2,0:T(8,128)} fusion(f32[6,8,384,64]{2,3,1,0:T(8,128)} %fusion.25, f32[6,384,8]{1,2,0:T(8,128)S(1)} %get-tuple-element.199, f32[6,8,64]{2,1,0:T(8,128)S(1)} %copy-done.31, bf16[6,384,8,64]{1,3,2,0:T(8,128)(2,1)} %copy-done.6, f32[6,8,384,384]{2,3,1,0:T(8,128)} %fusion.27, f32[6,8,384]{2,1,0:T(8,128)S(1)} %bitcast_multiply_fusion, ...), kind=kOutput, calls=%fused_computation.48 | convolution fusion | flops 5453512704 | bytes 40857600 | tf_op jit(solution)/shard_map/rhts,rshd->rthd/dot_general | solution.py:186
  416.9 8.1 copy.171
  425.0 9.0 reshape.289
  434.0 4.2 fusion.40
  438.2 51.9 %all-gather.3 = f32[48,8,64]{2,1,0:T(8,128)S(1)} all-gather(f32[6,8,64]{2,1,0:T(8,128)S(1)} %bitcast.171), channel_id=5, replica_groups=mesh['dp'=4,'seq'=8] {'seq'}, dimensions={0}, use_global_device_ids=true | all-gather | bytes 110592 | tf_op jit(solution)/shard_map/all_gather | solution.py:21
  490.1 4.9 fusion.63
  495.0 4.0 convert_reduce_fusion.5
  502.8 7.7 fusion.46
  510.6 34.6 %fusion.2 = f32[6,8,64,384]{3,2,1,0:T(8,128)} fusion(f32[6,8,384,384]{2,3,1,0:T(8,128)} %get-tuple-element.210, f32[384,384]{0,1:T(8,128)S(1)} %copy-done.13, f32[6,384,8]{1,2,0:T(8,128)S(1)} %get-tuple-element.200, f32[6,384,8,64]{1,0,3,2:T(8,128)} %reshape.276), kind=kOutput, calls=%fused_computation.8 | convolution fusion | flops 5444075520 | bytes 38412288 | tf_op jit(solution)/shard_map/rhts,rthe->rshe/dot_general | solution.py:192
  545.2 9.7 %fusion.64 = f32[2048,512]{1,0:T(8,128)} fusion(bf16[2304,2048]{1,0:T(8,128)(2,1)} %get-tuple-element.195, bf16[2304,512]{1,0:T(8,128)(2,1)} %bitcast.151), kind=kOutput, calls=%fused_computation.141 | convolution fusion | flops 4831838208 | bytes 15990784 | tf_op jit(solution)/shard_map/dot_general | solution.py:52
  554.9 16.1 %all-gather.9.cloned.1.call-done = f32[48,8,64,64]{3,2,1,0:T(8,128)} async-done(((f32[6,8,64,64]{3,2,1,0:T(8,128)}), f32[48,8,64,64]{3,2,1,0:T(8,128)}) %all-gather.9.cloned.1.call-update) | async-done | bytes 6291472 | tf_op jit(solution)/shard_map/all_gather | solution.py:21
  571.1 13.6 %while.27 = (s32[]{:T(128)}, f32[6,8,64,64]{3,2,1,0:T(8,128)S(1)}, f32[6,8,64]{2,1,0:T(8,128)S(1)}, s32[]{:T(128)}, f32[8,6,8,64,64]{4,3,2,1,0:T(8,128)}, /*inde...) while((s32[]{:T(128)}, f32[6,8,64,64]{3,2,1,0:T(8,128)S(1)}, ...), condition=%wide.region_12.13_spmd, body=%wide.region_11.12_spmd.sunk | while | flops 199686 | bytes 2396315 | solution.py:30
  584.7 5.9 fusion.59
  590.6 4.8 convert_reduce_fusion.3
  598.9 22.6 %fusion.19 = f32[6,384,8,64]{1,3,2,0:T(8,128)} fusion(f32[6,8,384,64]{2,3,1,0:T(8,128)} %fusion.59, f32[6,8,64]{2,1,0:T(8,128)S(1)} %get-tuple-element.137, bf16[6,384,8,64]{1,3,2,0:T(8,128)(2,1)} %copy.131, f32[6,8,384,384]{2,3,1,0:T(8,128)} %fusion.27, f32[6,8,384]{2,1,0:T(8,128)S(1)} %bitcast_multiply_fusion, f32[384,384]{0,1:T(8,128)S(1)} %copy-done.13), kind=kOutput, calls=%fused_computation.46 | convolution fusion | flops 5452333056 | bytes 40783872 | tf_op jit(solution)/shard_map/rhts,rthd->rshd/dot_general | solution.py:189
  621.5 8.1 copy.172
  629.6 9.0 reshape.290
  638.6 4.7 convert_reduce_fusion.4
  652.3 38.8 %pmax.7 = f32[]{:T(128)} all-reduce(f32[]{:T(128)S(6)} %div.77), channel_id=1, replica_groups=mesh['dp'=4,'seq'=8] {'dp','seq'}, use_global_device_ids=true, to_apply=%region_16.17 | all-reduce | flops 1 | bytes 8 | tf_op jit(solution)/shard_map/pmax | solution.py:141
  691.2 5.5 fusion.58
  696.7 11.2 %add_convert_fusion.4 = bf16[2304,512]{1,0:T(8,128)(2,1)} fusion(f32[2304,512]{1,0:T(8,128)} %copy-done.17, bf16[2304,2048]{1,0:T(8,128)(2,1)} %get-tuple-element.195, bf16[2048,512]{1,0:T(8,128)(2,1)S(1)} %copy-done.75, f32[512]{0:T(512)S(1)} %convert_element_type.154), kind=kOutput, calls=%fused_computation.67 | convolution fusion | flops 4835377152 | bytes 18614272 | tf_op jit(solution)/shard_map/dot_general | solution.py:48
  708.0 4.7 convolution_add_fusion.1
  718.2 45.0 %all-reduce = (f32[512]{0:T(512)}, f32[512]{0:T(512)}, f32[512]{0:T(512)}, f32[512]{0:T(512)}, f32[512]{0:T(512)}, /*index=5*/f32[512]{0:T(512)}, f32[512]{0:T(512)}, f32[512]{0:T(512)}, f32[2048]{0:T(1024)}, f32[512]{0:T(512)}) all-reduce(f32[512]{0:T(512)S(1)} %get-tuple-element.140, ...), channel_id=1, replica_groups=mesh['dp'=4,'seq'=8] {'dp','seq'}, use_global_device_ids=true, to_apply=%region_18.19 | all-reduce | flops 6656 | bytes 53248 | tf_op jit(solution)/shard_map/psum | solution.py:217
  763.2 7.8 add_convert_fusion.2
  771.0 114.4 %all-reduce.4.cloned.1.call-done = (f32[512,512]{1,0:T(8,128)}, f32[512,512]{1,0:T(8,128)}, f32[512,512]{1,0:T(8,128)}, f32[512,512]{1,0:T(8,128)}, f32[512,2048]{1,0:T(8,128)}, /*index=5*/f32[2048,512]{1,0:T(8,128)}) async-done(((f32[512,512]{1,0:T(8,128)}, f32[512,512]{1,0:T(8,128)}, f32[512,512]{1,0:T(8,128)}, f32[512,512]{1,0:T(8,128)}, f32[512,2048]{1,0:T(8,128)}, /*index=5*/f32[2048,512]{1,0:T(8,128)}), ...) | async-done | bytes 12582928 | tf_op jit(solution)/shard_map/psum | solution.py:217
  (260 shorter events, 84.0 us)
Async XLA Ops:
  7.2 253.7 %copy-start = (bf16[512,2048]{1,0:T(8,128)(2,1)S(1)}, bf16[512,2048]{1,0:T(8,128)(2,1)}, u32[]{:S(2)}) copy-start(bf16[512,2048]{1,0:T(8,128)(2,1)} %param.37) | copy-start | bytes 6291460
  7.2 7.7 copy-start.43
  7.2 235.7 %all-gather.7.cloned.1.call-start = ((), (), s32[]{:S(2)}) async-start(), calls=%async_computation | async-start | bytes 14155776 | tf_op jit(solution)/shard_map/all_gather | solution.py:21
  12.1 8.4 copy-start.45
  12.2 8.4 copy-start.53
  12.2 8.4 copy-start.49
  12.2 105.3 %copy-start.57 = (f32[512]{0:T(512)}, f32[512]{0:T(512)S(1)}, u32[]{:S(2)}) copy-start(f32[512]{0:T(512)S(1)} %convert_element_type.135) | copy-start | bytes 6148
  14.9 5.6 copy-start.25
  28.5 8.9 copy-start.69
  28.5 8.9 copy-start.41
  62.0 509.0 %all-gather.9.cloned.1.call-start = ((), (), s32[]{:S(2)}) async-start(), calls=%async_computation.1 | async-start | bytes 14155776 | tf_op jit(solution)/shard_map/all_gather | solution.py:21
  75.8 6.5 copy-start.71
  75.8 6.5 copy-start.72
  75.8 6.5 copy-start.63
  75.8 6.5 copy-start.73
  83.6 37.4 %copy-start.4 = (bf16[6,384,8,64]{1,3,2,0:T(8,128)(2,1)S(1)}, bf16[6,384,8,64]{1,3,2,0:T(8,128)(2,1)}, u32[]{:S(2)}) copy-start(bf16[6,384,8,64]{1,3,2,0:T(8,128)(2,1)} %copy.131) | copy-start | bytes 7077892
  83.6 37.4 %copy-start.7 = (bf16[6,384,8,64]{1,3,2,0:T(8,128)(2,1)S(1)}, bf16[6,384,8,64]{1,3,2,0:T(8,128)(2,1)}, u32[]{:S(2)}) copy-start(bf16[6,384,8,64]{1,3,2,0:T(8,128)(2,1)} %copy-done.6) | copy-start | bytes 7077892
  117.5 15.0 %copy-start.12 = (f32[384,384]{0,1:T(8,128)}, f32[384,384]{0,1:T(8,128)S(1)}, u32[]{:S(2)}) copy-start(f32[384,384]{0,1:T(8,128)S(1)} %fusion.35) | copy-start | bytes 1769476
  132.4 114.8 %copy-start.33 = (f32[6,8,384]{2,1,0:T(8,128)}, f32[6,8,384]{2,1,0:T(8,128)S(1)}, u32[]{:S(2)}) copy-start(f32[6,8,384]{2,1,0:T(8,128)S(1)} %get-tuple-element.209) | copy-start | bytes 221188
  244.3 11.8 %copy-start.30 = (f32[6,8,64]{2,1,0:T(8,128)}, f32[6,8,64]{2,1,0:T(8,128)S(1)}, u32[]{:S(2)}) copy-start(f32[6,8,64]{2,1,0:T(8,128)S(1)} %get-tuple-element.135) | copy-start | bytes 36868
  247.3 8.8 copy-start.35
  247.9 8.2 copy-start.47
  259.8 82.2 %copy-start.17 = (f32[2304,512]{1,0:T(8,128)}, f32[2304,512]{1,0:T(8,128)S(1)}, u32[]{:S(2)}) copy-start(f32[2304,512]{1,0:T(8,128)S(1)} %get-tuple-element.214) | copy-start | bytes 14155780
  260.8 49.0 %copy-start.51 = (f32[2304]{0:T(1024)}, f32[2304]{0:T(1024)S(1)}, u32[]{:S(2)}) copy-start(f32[2304]{0:T(1024)S(1)} %multiply_reduce_fusion.6) | copy-start | bytes 27652
  260.8 49.0 %copy-start.16 = (bf16[6,384,512]{2,1,0:T(8,128)(2,1)S(1)}, bf16[6,384,512]{2,1,0:T(8,128)(2,1)}, u32[]{:S(2)}) copy-start(bf16[6,384,512]{2,1,0:T(8,128)(2,1)} %param.41) | copy-start | bytes 7077892
  331.7 10.3 %copy-start.52 = (f32[2304]{0:T(1024)S(1)}, f32[2304]{0:T(1024)}, u32[]{:S(2)}) copy-start(f32[2304]{0:T(1024)} %copy-done.51) | copy-start | bytes 27652
  358.3 5.8 slice-start
  358.3 5.8 copy-start.48
  358.3 6.1 slice-start.1
  358.3 6.8 copy-start.5
  369.7 515.7 %all-reduce.4.cloned.1.call-start = ((), (), s32[]{:S(2)}) async-start(), calls=%async_computation.2 | async-start | bytes 25165824 | tf_op jit(solution)/shard_map/psum | solution.py:217
  369.8 9.2 %copy-start.11 = (bf16[6,384,8,64]{1,3,2,0:T(8,128)(2,1)S(1)}, bf16[6,384,8,64]{1,3,2,0:T(8,128)(2,1)}, u32[]{:S(2)}) copy-start(bf16[6,384,8,64]{1,3,2,0:T(8,128)(2,1)} %copy.132) | copy-start | bytes 7077892
  379.0 18.5 %copy-start.13 = (f32[384,384]{0,1:T(8,128)S(1)}, f32[384,384]{0,1:T(8,128)}, u32[]{:S(2)}) copy-start(f32[384,384]{0,1:T(8,128)} %copy-done.12) | copy-start | bytes 1769476
  379.0 18.5 %copy-start.31 = (f32[6,8,64]{2,1,0:T(8,128)S(1)}, f32[6,8,64]{2,1,0:T(8,128)}, u32[]{:S(2)}) copy-start(f32[6,8,64]{2,1,0:T(8,128)} %copy-done.30) | copy-start | bytes 36868
  438.2 56.8 %slice-start.2 = ((s8[4718592]{0:T(1024)(128)(4,1)}), s8[4194304]{0:T(1024)(128)(4,1)S(1)}, s32[]{:S(2)}) async-start(s8[4718592]{0:T(1024)(128)(4,1)} %bitcast.153), calls=%async_computation.5 | async-start | bytes 8388608
  490.1 12.7 %slice-start.4 = ((s8[4718592]{0:T(1024)(128)(4,1)}), s8[4194304]{0:T(1024)(128)(4,1)S(1)}, s32[]{:S(2)}) async-start(s8[4718592]{0:T(1024)(128)(4,1)} %bitcast.155), calls=%async_computation.7 | async-start | bytes 8388608
  495.0 7.8 slice-start.5
  495.0 7.8 slice-start.6
  495.0 7.8 slice-start.7
  584.7 5.9 copy-start.8
  638.6 6.2 copy-start.27
  649.5 41.7 %copy-start.40 = (bf16[512,512]{1,0:T(8,128)(2,1)S(1)}, bf16[512,512]{1,0:T(8,128)(2,1)}, u32[]{:S(2)}) copy-start(bf16[512,512]{1,0:T(8,128)(2,1)} %param.27) | copy-start | bytes 1572868
  691.2 5.5 copy-start.75
  696.7 11.3 %copy-start.44 = (bf16[512,512]{1,0:T(8,128)(2,1)S(1)}, bf16[512,512]{1,0:T(8,128)(2,1)}, u32[]{:S(2)}) copy-start(bf16[512,512]{1,0:T(8,128)(2,1)} %param.29) | copy-start | bytes 1572868
  715.5 47.7 %copy-start.56 = (f32[2304]{0:T(1024)S(1)}, f32[2304]{0:T(1024)}, u32[]{:S(2)}) copy-start(f32[2304]{0:T(1024)} %copy-done.55) | copy-start | bytes 27652
  885.4 6.9 copy-start.32
  885.4 7.9 copy-start.24
  893.3 5.7 copy-start.1
  (40 other events, 138.8 us)
Sparse Core Ops, SparseCore 0:
  62.1 180.7 all-gather.6
  369.8 201.0 all-gather.8
  649.7 235.6 all-reduce.3
where the time goes:
time: 917 us; the launch traced here: 906 us
  matrix products  322 us (35%)
  waiting for transfers between devices  224 us (24%)
  blocking collectives  170 us (19%)
  local copies, waits for them, and re-layouts  113 us (12%)
  other arithmetic  60.6 us (7%)
  between operations  16.4 us (2%)
    psum x1, waiting for transfers between devices, per_device(): summed = lax.psum(attn_grads + ffn_grads, ('dp', 'seq'))  114 us
    all_gather x2, waiting for transfers between devices, entering(): gathered = jax.tree.map(lambda a: lax.all_gather(a, axis), part)  109 us
    all_gather x2, blocking collectives, entering(): gathered = jax.tree.map(lambda a: lax.all_gather(a, axis), part)  85.7 us
    dot_general x6, matrix products, matmul(): return jnp.dot(left, right, preferred_element_type=jnp.float32)  78.6 us
    dot_general x6, matrix products, times_transposed(): lax.dot_general(left, right, (((1,), (1,)), ((), ())), preferred_element_...  48.7 us
    psum x1, blocking collectives, per_device(): summed = lax.psum(attn_grads + ffn_grads, ('dp', 'seq'))  45 us
    pmax x1, blocking collectives, per_device(): den_peak = lax.pmax(local_peak, ('dp', 'seq'))  38.8 us
    dot_general x1, matrix products, per_device(): jnp.einsum('rhts,rthe->rshe', scores, numer_grad, precision=HIGH)  34.6 us
  transfers between devices with their start and end apart: 3, of which 3 were waited for; matrix products, arithmetic and copies ran while one was open for 25% of the time, Pallas kernels for 0%

commit v1 on v0

v1 whole, which is shorter than its diff:
```python
import functools

import jax
import jax.numpy as jnp
from jax import lax
from jax.experimental import pallas as pl
from jax.experimental.pallas import tpu as pltpu
from jax.sharding import PartitionSpec as P

HEADS = 8
LEN_LONG = 3072
LEN_SHORT = 784
EPSILON = 1e-05
F32, BF16 = jnp.float32, jnp.bfloat16
MESH = pl.DeviceIdType.MESH

WIDTH = 512
PART = 512
QUAD = 256
DEPTH = 64
HALVINGS = 3
CHUNK = 1024
CHUNKS = 6
LANDS = 5
SHARES = (4, 3, 1)
VECS = 16
FIRST_LIMIT = 16


def mm(a, b):
    return lax.dot_general(a, b, (((1,), (0,)), ((), ())), preferred_element_type=F32)


def nt(a, b):
    return lax.dot_general(a, b, (((1,), (1,)), ((), ())), preferred_element_type=F32)


def tn(a, b):
    return lax.dot_general(a, b, (((0,), (0,)), ((), ())), preferred_element_type=F32)


def colsum(v):
    return jnp.sum(v, axis=0, keepdims=True)


def bit(index, step):
    return lax.rem(lax.div(index, step), 2)


def aligned(v, m=8):
    return v if isinstance(v, int) else pl.multiple_of(v, m)


def coord(dim):
    return bit(lax.axis_index(dim[0]), dim[1])


def peer(dim):
    axis, step = dim
    d, s = lax.axis_index("dp"), lax.axis_index("seq")
    if axis == "dp":
        return (d + step * (1 - 2 * bit(d, step)), s)
    return (d, s + step * (1 - 2 * bit(s, step)))


def remote(src, dst, send, recv, device):
    return pltpu.make_async_remote_copy(
        src_ref=src, dst_ref=dst, send_sem=send, recv_sem=recv, device_id=device, device_id_type=MESH
    )


class Reduce:
    def __init__(self, dims, orders):
        self.core, self.orders = ("dp", 1), orders
        self.half = CHUNK // 2
        unit = self.half // sum(SHARES)
        self.sizes = [unit * s for s in SHARES]
        self.starts = [sum(self.sizes[:i]) for i in range(len(SHARES))]
        self.whole = len(dims) - HALVINGS
        self.between = 2 * HALVINGS + self.whole
        self.steps = self.between + 3
        self.sems = 2 + len(SHARES) * self.between
        self.frees = 1 + len(SHARES) * HALVINGS
        self.bases = [self.half]
        for p in range(len(SHARES)):
            self.bases.append(self.bases[-1] + self.offset(p, HALVINGS + self.whole))
        self.rows = self.bases[-1]

    def offset(self, p, k):
        n = self.sizes[p]
        over = max(k - HALVINGS, 0)
        return n - (n >> min(k, HALVINGS)) + over * (n >> HALVINGS)

    def piece(self, p, k):
        at = coord(self.core) * self.half + self.starts[p]
        for i in range(k):
            at = at + coord(self.orders[p][i]) * (self.sizes[p] >> (i + 1))
        return at

    def copies(self, g, r, ss, rs, stage):
        half = self.half
        if stage in (0, self.steps - 2):
            c = coord(self.core)
            mine, other = aligned(c * half), aligned((1 - c) * half)
            if stage == 0:
                dst = r.at[pl.ds(0, half)]
                cp = remote(g.at[pl.ds(other, half)], dst, ss.at[0], rs.at[0], peer(self.core))
                return [(cp, mine, 0, half, 0, peer(self.core))]
            part = g.at[pl.ds(mine, half)]
            cp = remote(part, part, ss.at[1], rs.at[1], peer(self.core))
            return [(cp, None, None, half, 0, peer(self.core))]
        out = []
        k = stage - 1
        for p, order in enumerate(self.orders):
            n = self.sizes[p]
            sem = 2 + p * self.between + k
            land = self.bases[p] + self.offset(p, k)
            free = None
            if k < HALVINGS:
                free = 1 + p * HALVINGS + k
                m, dim, base = n >> (k + 1), order[k], self.piece(p, k)
                c = coord(dim)
                src = g.at[pl.ds(aligned(base + (1 - c) * m), m)]
                dst, to = r.at[pl.ds(land, m)], aligned(base + c * m)
            elif k < HALVINGS + self.whole:
                m, dim, to = n >> HALVINGS, order[k], aligned(self.piece(p, HALVINGS))
                src, dst = g.at[pl.ds(to, m)], r.at[pl.ds(land, m)]
            else:
                i = self.between - 1 - k
                free = 1 + p * HALVINGS + i
                m, dim, to, land = n >> (i + 1), order[i], None, None
                src = dst = g.at[pl.ds(aligned(self.piece(p, i + 1)), m)]
            cp = remote(src, dst, ss.at[sem], rs.at[sem], peer(dim))
            out.append((cp, to, land, m, free, peer(dim)))
        return out

    def step(self, g, r, ss, rs, fs, k):
        if k > 0:
            for cp, to, land, m, free, device in self.copies(g, r, ss, rs, k - 1):
                cp.wait()
                if to is not None:
                    slab = next(s for s in (64, 48, 32, 24, 16, 8) if m % s == 0)

                    def one(i, c, to=to, land=land, slab=slab):
                        a = pl.ds(pl.multiple_of(to + i * slab, 8), slab)
                        g[a, :] += r[pl.ds(pl.multiple_of(land + i * slab, 8), slab), :]
                        return c

                    lax.fori_loop(0, m // slab, one, 0)
                    if free is not None:
                        pl.semaphore_signal(fs.at[free], inc=1, device_id=device, device_id_type=MESH)
        if k < self.steps - 1:
            for cp, to, _, _, free, _ in self.copies(g, r, ss, rs, k):
                if to is None:
                    pl.semaphore_wait(fs.at[free], 1)
                cp.start()


class Scan:
    def __init__(self, seq, back, own, rx1, rxp, txp, tx2, rx2, prior, ss, rs):
        self.hops = seq // 2
        place = lax.axis_index("seq")
        self.dp, self.place = lax.axis_index("dp"), place
        lo, hi = lax.rem(place, 2), lax.div(place, 2)
        self.partner = (self.dp, place + 1 - 2 * lo)
        self.next = (self.dp, place - 2 if back else place + 2)
        self.lo = 1 - lo if back else lo
        self.hi = self.hops - 1 - hi if back else hi
        self.own, self.rx1, self.rxp, self.txp = own, rx1, rxp, txp
        self.tx2, self.rx2, self.prior, self.ss, self.rs = tx2, rx2, prior, ss, rs

    def first(self, b):
        src = self.own.at[b, 1 - self.lo]
        return remote(src, self.rx1.at[b], self.ss.at[b, 0], self.rs.at[b, 0], self.partner)

    def chain(self, b):
        return remote(
            self.txp.at[b], self.rxp.at[b], self.ss.at[b, 1], self.rs.at[b, 1], self.next
        )

    def last(self, b):
        return remote(
            self.tx2.at[b], self.rx2.at[b], self.ss.at[b, 2], self.rs.at[b, 2], self.partner
        )

    def begin(self, b):
        self.first(b).start()

    def hop(self, b):
        @pl.when(self.hi == 0)
        def _():
            self.rxp[b] = jnp.zeros_like(self.rxp[b])

        self.first(b).wait()
        mine = self.own[b, self.lo]
        other = self.rx1[b]

        @pl.when(self.hi > 0)
        def _():
            self.chain(b).wait_recv()

        came = self.rxp[b]

        @pl.when(self.hi < self.hops - 1)
        def _():
            self.txp[b] = came + mine + other
            self.chain(b).start()

        upper = self.lo.astype(F32)
        self.tx2[b] = came + (1.0 - upper) * mine
        self.last(b).start()
        self.prior[b, self.lo] = came + upper * other

    def end(self, b):
        self.last(b).wait()

        @pl.when(self.hi < self.hops - 1)
        def _():
            self.chain(b).wait_send()

        self.prior[b, 1 - self.lo] = self.rx2[b]


def norm_parts(v):
    centre = v - jnp.mean(v, axis=-1, keepdims=True)
    rate = lax.rsqrt(jnp.mean(centre * centre, axis=-1, keepdims=True) + EPSILON)
    return centre * rate, rate


def norm_back(grad, unit, rate, gain):
    inner = grad * gain
    shift = jnp.mean(inner, axis=-1, keepdims=True)
    scale = jnp.mean(inner * unit, axis=-1, keepdims=True)
    return rate * (inner - shift - unit * scale)


def feature(v):
    return jnp.where(v > 0, v + 1.0, jnp.exp(jnp.minimum(v, 0.0)))


def normal_parts(u):
    e = jnp.exp(-0.5 * u * u)
    t = 1.0 / (1.0 + 0.3275911 * 0.7071067811865476 * jnp.abs(u))
    poly = 1.421413741 + t * (-1.453152027 + t * 1.061405429)
    poly = t * (0.254829592 + t * (-0.284496736 + t * poly))
    tail = 0.5 * poly * e
    return jnp.where(u > 0, 1.0 - tail, tail), e * 0.3989422804014327


def split(v):
    high = v.astype(BF16)
    return high, (v - high.astype(F32)).astype(BF16)


def four(v):
    return jnp.concatenate([v] * 4, axis=0)


def fold(v):
    return v[0:64] + v[64:128] + v[128:192] + v[192:256]


N1G, N1B, QB, KB, VB, OB, N2G, N2B, RB, HB, PEAK = range(11)
PEAK = 13


def kernel(
    seq,
    images,
    span,
    red,
    dims,
    tok_hbm,
    cot_hbm,
    vec,
    wq_hbm,
    wk_hbm,
    wv_hbm,
    wo_hbm,
    w1_hbm,
    w2_hbm,
    lay_hbm,
    ing_hbm,
    gw2_hbm,
    gw1_hbm,
    gwo_hbm,
    gwq_hbm,
    gwk_hbm,
    gwv_hbm,
    sums_ref,
    x,
    ct,
    fq,
    fk,
    vb,
    at,
    iv,
    si,
    out,
    d2,
    ws,
    w1,
    w2,
    g,
    sb,
    srx,
    own,
    rx1,
    f_rxp,
    b_rxp,
    txp,
    tx2,
    rx2,
    f_prior,
    b_prior,
    mu,
    mx,
    bo,
    bof,
    cm,
    cmt,
    in_sem,
    w_sem,
    out_sem,
    go_sem,
    red_ss,
    red_rs,
    red_fs,
    f_ss,
    f_rs,
    b_ss,
    b_rs,
    s_ss,
    s_rs,
):
    per = 2 if images % 2 == 0 else 1
    blocks = images // per
    rows = per * span
    size = 128 if span % 128 == 0 else span
    parts = span // size
    place = lax.axis_index("seq")

    def block(b):
        return pl.ds(pl.multiple_of(b * rows, 16), rows)

    def image(b, im):
        return pl.ds(pl.multiple_of(b * rows + im * span, 16), span)

    def spot(b, im, c):
        return pl.ds(pl.multiple_of(b * rows + im * span + c * size, 16), size)

    def fetch(hbm, ref, sem, b):
        return pltpu.make_async_copy(hbm.at[block(b)], ref.at[block(b)], sem.at[b])

    for b in range(blocks):
        fetch(tok_hbm, x, in_sem.at[0], b).start()
    loads = [pltpu.make_async_copy(h, ws.at[i], w_sem.at[i]) for i, h in enumerate((wq_hbm, wk_hbm, wv_hbm, wo_hbm))]
    def weights(j):
        cols = pl.ds(j * PART, PART)
        return (
            pltpu.make_async_copy(w1_hbm.at[:, cols], w1.at[j % 2], w_sem.at[4 + j]),
            pltpu.make_async_copy(w2_hbm.at[cols, :], w2.at[j % 2], w_sem.at[8 + j]),
        )

    def fill(j):
        for load in weights(j):
            load.start()

    def filled(j):
        for load in weights(j):
            load.wait()

    for load in loads:
        load.start()
    fill(0)
    fill(1)
    for b in range(blocks):
        fetch(cot_hbm, ct, in_sem.at[1], b).start()

    barrier = pltpu.get_barrier_semaphore()
    chain = [(lax.axis_index("dp"), lax.rem(place + d, seq)) for d in (2, seq - 2)]
    friends = [peer(d) for d in [("dp", 1)] + dims] + chain
    for friend in friends:
        pl.semaphore_signal(barrier, inc=1, device_id=friend, device_id_type=MESH)

    same = lax.broadcasted_iota(jnp.int32, (QUAD, QUAD), 0) // DEPTH == lax.broadcasted_iota(jnp.int32, (QUAD, QUAD), 1) // DEPTH
    bof[...] = jnp.where(same, 1.0, 0.0)
    bo[...] = bof[...].astype(BF16)
    same = lax.broadcasted_iota(jnp.int32, (4 * size, QUAD), 0) // size == lax.broadcasted_iota(jnp.int32, (4 * size, QUAD), 1) // DEPTH
    mx[...] = jnp.where(same, 1.0, 0.0).astype(BF16)
    t = lax.broadcasted_iota(jnp.int32, (size, 4 * size), 0)
    s = lax.broadcasted_iota(jnp.int32, (size, 4 * size), 1) % size
    cm[...] = jnp.where(s <= t, 1.0, 0.0)
    cmt[...] = jnp.where(s >= t, 1.0, 0.0)
    sb[...] = jnp.zeros_like(sb)

    def clear(i, c):
        def inner(k, c):
            g[i, pl.ds(pl.multiple_of(k * 64, 8), 64), :] = jnp.zeros((64, WIDTH), F32)
            return c

        return lax.fori_loop(0, CHUNK // 64, inner, c)

    lax.fori_loop(0, LANDS, clear, 0)

    def row(i):
        return vec[i : i + 1, :]

    def add(i, v):
        sb[i : i + 1, :] += v

    def limit(b, im):
        return vec[pl.ds(FIRST_LIMIT + b * per + im, 1), :]

    def positions(start, count, width):
        return (lax.broadcasted_iota(jnp.int32, (count, width), 0) + (place * span + start)).astype(F32)

    forward = Scan(seq, False, own, rx1, f_rxp, txp, tx2, rx2, f_prior, f_ss, f_rs)
    backward = Scan(seq, True, own, rx1, b_rxp, txp, tx2, rx2, b_prior, b_ss, b_rs)

    for i in range(3):
        loads[i].wait()

    def phase_a(b, c):
        fetch(tok_hbm, x, in_sem.at[0], b).wait()
        pos = positions(0, span, WIDTH)
        for im in range(per):
            part = image(b, im)
            unit, _ = norm_parts(x[part, :].astype(F32))
            first = (unit * row(N1G) + row(N1B)).astype(BF16)
            fq[part, :] = feature(mm(first, ws[0]) + row(QB)).astype(BF16)
            key = feature(mm(first, ws[1]) + row(KB))
            key = jnp.where(pos < limit(b, im), key, 0.0).astype(BF16)
            fk[part, :] = key
            value = (mm(first, ws[2]) + row(VB)).astype(BF16)
            vb[part, :] = value
            total = colsum(key.astype(F32))
            for q in range(2):
                cols = slice(q * QUAD, (q + 1) * QUAD)
                state = fold(tn(key[:, cols], value[:, cols]) * bof[...])
                own[b, q, im * 64 : im * 64 + 64, :] = state
                own[b, q, per * 64 + im : per * 64 + im + 1, :] = total[:, cols]

        @pl.when(b == 0)
        def _():
            pl.semaphore_wait(barrier, len(friends))

        forward.begin(b)
        return c

    for q in range(2):
        for b in range(blocks):
            own[b, q, per * 64 : per * 64 + 8, :] = jnp.zeros((8, QUAD), F32)
    lax.fori_loop(0, blocks, phase_a, 0)

    def hops(scan):
        def one(b, c):
            scan.hop(b)
            return c

        lax.fori_loop(0, blocks, one, 0)

    hops(forward)
    loads[3].wait()
    filled(0)

    def known(ref, b, im, q):
        state = ref[b, q, pl.ds(pl.multiple_of(im * 64, 8), 64), :]
        return four(state) * bof[...], ref[b, q, pl.ds(per * 64 + im, 1), :]

    def entering(b, im, q):
        cols = slice(q * QUAD, (q + 1) * QUAD)
        state, total = known(f_prior, b, im, q)
        states, totals = [], []
        for c in range(parts):
            states.append(split(state))
            totals.append(total)
            if c < parts - 1:
                key = fk[spot(b, im, c), cols]
                state = state + tn(key, vb[spot(b, im, c), cols]) * bof[...]
                total = total + colsum(key.astype(F32))
        return states, totals

    def each(im, q):
        return [(im, q, c) for c in range(parts)]

    def read(ref, b, one):
        im, q, c = one
        return ref[spot(b, im, c), q * QUAD : (q + 1) * QUAD]

    def write(ref, b, one, v):
        im, q, c = one
        ref[spot(b, im, c), q * QUAD : (q + 1) * QUAD] = v

    def centre(b, im, q):
        return mu[pl.ds(b * per + im, 1), q * QUAD : (q + 1) * QUAD]

    def head_sums(v):
        high, low = split(v)
        return mm(high, bo[...]) + mm(low, bo[...])

    def attend(b, im):
        for q in range(2):
            near = pl.ds(pl.multiple_of(im * 64, 8), 64)
            count = f_prior[b, q, pl.ds(per * 64 + im, 1), :] + own[b, q, pl.ds(per * 64 + im, 1), :]
            count = head_sums(jnp.broadcast_to(count, (8, QUAD)))[0:1]
            off = colsum(f_prior[b, q, near, :] + own[b, q, near, :]) / count
            mu[pl.ds(b * per + im, 1), q * QUAD : (q + 1) * QUAD] = off
            ones = each(im, q)
            states, totals = entering(b, im, q)
            query = [read(fq, b, o) for o in ones]
            score = [(nt(u, four(read(fk, b, o)) * mx[...]) * cm[...]).astype(BF16) for u, o in zip(query, ones)]
            num = [mm(v, four(read(vb, b, o)) * mx[...]) for v, o in zip(score, ones)]
            den = [mm(v, mx[...]) for v in score]
            cols = slice(q * QUAD, (q + 1) * QUAD)
            for c, o in enumerate(ones):
                n = num[c] + mm(query[c], states[c][0]) + mm(query[c], states[c][1])
                d = den[c] + head_sums(query[c].astype(F32) * totals[c])
                inverse = 1.0 / d
                write(at, b, o, (n * inverse - off).astype(BF16))
                write(iv, b, o, inverse.astype(BF16))
                inside = positions(c * size, size, QUAD) < limit(b, im)[:, cols]
                peak = jnp.max(jnp.where(inside, d, 0.0), axis=0, keepdims=True)
                sb[PEAK : PEAK + 1, cols] = jnp.maximum(sb[PEAK : PEAK + 1, cols], peak)

    def uncentred(den_grad, num_grad, off):
        return den_grad.astype(F32) - head_sums(num_grad.astype(F32) * off)

    def attended(b, im):
        return (at[image(b, im), :].astype(F32) + mu[pl.ds(b * per + im, 1), :]).astype(BF16)

    def feed(j, b):
        normed, grad = si[block(b), :], ct[block(b), :]
        up, down = w1[lax.rem(j, 2)], w2[lax.rem(j, 2)]
        act, pre = [], []
        for im in range(per):
            part = slice(im * span, (im + 1) * span)
            hidden = mm(normed[part], up) + vec[pl.ds(HB + j, 1), :]
            back = nt(grad[part], down)
            cdf, pdf = normal_parts(hidden)
            act.append((hidden * cdf).astype(BF16))
            pre.append((back * (cdf + hidden * pdf)).astype(BF16))
            out[image(b, im), :] += mm(act[im], down)
            d2[image(b, im), :] += nt(pre[im], up)
        act, pre = jnp.concatenate(act, axis=0), jnp.concatenate(pre, axis=0)
        g[j, 0:512, :] += tn(act, grad)
        g[j, 512:1024, :] += tn(normed, pre)
        sb[pl.ds(HB + j, 1), :] += colsum(pre.astype(F32))

    def store(c, i):
        if i == 0:
            return pltpu.make_async_copy(g.at[c, pl.ds(0, 512)], gw2_hbm.at[pl.ds(pl.multiple_of(c * PART, PART), PART), :], go_sem.at[c, 0])
        return pltpu.make_async_copy(g.at[c, pl.ds(512, 512)], gw1_hbm.at[:, pl.ds(pl.multiple_of(c * PART, PART), PART)], go_sem.at[c, 1])

    times = red_times(red.steps)

    def tick(t):
        for k in reversed(range(red.steps)):
            ahead = t - times[k]
            c = lax.div(ahead, 3)

            @pl.when(jnp.logical_and(ahead >= 0, jnp.logical_and(lax.rem(ahead, 3) == 0, c < 4)))
            def _(k=k, c=c):
                red.step(g.at[c], g.at[LANDS + c], red_ss.at[c], red_rs.at[c], red_fs.at[c], k)
                if k == red.steps - 1:
                    store(c, 0).start()
                    store(c, 1).start()

    def phase_b(b, c):
        forward.end(b)
        def one(im, c):
            attend(b, im)
            return c

        lax.fori_loop(0, per, one, 0)
        for im in range(per):
            part = image(b, im)
            mid = x[part, :].astype(F32) + mm(attended(b, im), ws[3]) + row(OB)
            unit, _ = norm_parts(mid)
            si[part, :] = (unit * row(N2G) + row(N2B)).astype(BF16)
            out[part, :] = mid + row(RB)
        d2[block(b), :] = jnp.zeros((rows, WIDTH), F32)
        fetch(cot_hbm, ct, in_sem.at[1], b).wait()
        add(RB, colsum(ct[block(b), :].astype(F32)))
        feed(0, b)

        @pl.when(b == blocks - 1)
        def _():
            tick(0)

        return c

    lax.fori_loop(0, blocks, phase_b, 0)

    fill(2)
    filled(1)

    def phase_f(i, c):
        feed(1 + lax.div(i, blocks), lax.rem(i, blocks))

        @pl.when(i == blocks - 1)
        def _():
            fill(3)
            filled(2)

        tick(1 + i)
        return c

    lax.fori_loop(0, 2 * blocks, phase_f, 0)
    filled(3)
    tick0 = 1 + 2 * blocks

    def save(ref, hbm, b):
        return pltpu.make_async_copy(ref.at[block(b)], hbm.at[block(b)], out_sem.at[b])

    def phase_g(b, c):
        feed(3, b)
        def one(im, c):
            part = image(b, im)
            attn = attended(b, im)
            unit, rate = norm_parts(x[part, :].astype(F32) + mm(attn, ws[3]) + row(OB))
            grad = d2[part, :]
            add(N2G, colsum(grad * unit))
            add(N2B, colsum(grad))
            residual = ct[part, :].astype(F32) + norm_back(grad, unit, rate, row(N2G))
            d2[part, :] = residual
            ct[part, :] = out[part, :].astype(BF16)
            low = residual.astype(BF16)
            g[4, 0:512, :] += tn(attn, low)
            add(OB, colsum(low.astype(F32)))
            mixed_grad = nt(low, ws[3])
            inverse = iv[part, :].astype(F32)
            num_grad = (mixed_grad * inverse).astype(BF16)
            si[part, :] = num_grad
            inner = num_grad.astype(F32) * at[part, :].astype(F32)
            query = fq[part, :]
            for q in range(2):
                cols = slice(q * QUAD, (q + 1) * QUAD)
                den_grad = (-head_sums(inner[:, cols])).astype(BF16)
                iv[part, cols] = den_grad
                whole = uncentred(den_grad, num_grad[:, cols], centre(b, im, q))
                total = colsum(whole * query[:, cols].astype(F32))
                state = fold(tn(query[:, cols], num_grad[:, cols]) * bof[...])
                own[b, q, pl.ds(pl.multiple_of(im * 64, 8), 64), :] = state
                own[b, q, pl.ds(per * 64 + im, 1), :] = total
            return c

        lax.fori_loop(0, per, one, 0)
        save(ct, lay_hbm, b).start()
        backward.begin(b)
        tick(tick0 + b)
        return c

    lax.fori_loop(0, blocks, phase_g, 0)
    tick1 = tick0 + blocks

    @pl.when(backward.hi == 0)
    def _():
        hops(backward)

    def together(pieces):
        return jnp.concatenate([jnp.concatenate(p, axis=0) for p in pieces], axis=1)

    def less(b, one):
        return (read(vb, b, one).astype(F32) - centre(b, one[0], one[1])).astype(BF16)

    def query_side(b, im):
        unit, _ = norm_parts(x[image(b, im), :].astype(F32))
        first = (unit * row(N1G) + row(N1B)).astype(BF16)
        at[image(b, im), :] = first
        low = []
        for q in range(2):
            ones = each(im, q)
            states, totals = entering(b, im, q)
            num_grad = [read(si, b, o) for o in ones]
            den_grad = [read(iv, b, o) for o in ones]
            back = [
                ((nt(n, four(less(b, o)) * mx[...]) + nt(d, mx[...] * 0.015625)) * cm[...]).astype(BF16)
                for n, d, o in zip(num_grad, den_grad, ones)
            ]
            side = [mm(v, four(read(fk, b, o)) * mx[...]) for v, o in zip(back, ones)]
            pieces = []
            for c, o in enumerate(ones):
                whole = uncentred(den_grad[c], num_grad[c], centre(b, im, q))
                grad = side[c] + nt(num_grad[c], states[c][0]) + nt(num_grad[c], states[c][1])
                grad = grad + whole * totals[c]
                pieces.append((grad * jnp.minimum(read(fq, b, o).astype(F32), 1.0)).astype(BF16))
            low.append(pieces)
        low = together(low)
        g[4, 512:1024, :] += tn(first, low)
        add(QB, colsum(low.astype(F32)))
        out[image(b, im), :] = nt(low, ws[0])

    def phase_q(b, c):
        def one(im, c):
            query_side(b, im)
            return c

        lax.fori_loop(0, per, one, 0)
        due = jnp.logical_or(backward.hi == b + 1, jnp.logical_and(b == blocks - 1, backward.hi > blocks))

        @pl.when(due)
        def _():
            hops(backward)

        tick(tick1 + b)
        return c

    lax.fori_loop(0, blocks, phase_q, 0)
    tick2 = tick1 + blocks

    def chunk4(k):
        red.step(g.at[4], g.at[LANDS + 1], red_ss.at[1], red_rs.at[1], red_fs.at[1], k)

    def chunk5(k):
        red.step(g.at[5], g.at[LANDS + 2], red_ss.at[2], red_rs.at[2], red_fs.at[2], k)

    def key_side(b, im):
        first = at[image(b, im), :]
        share = jnp.full((size, QUAD), 0.015625, BF16)
        low_k, low_v = [], []
        for q in range(2):
            ones = each(im, q)
            cols = slice(q * QUAD, (q + 1) * QUAD)
            state, total = known(b_prior, b, im, q)
            states, totals = [], []
            for c in reversed(range(parts)):
                states.insert(0, split(state))
                totals.insert(0, total)
                if c > 0:
                    query, num_grad = fq[spot(b, im, c), cols], si[spot(b, im, c), cols]
                    state = state + tn(query, num_grad) * bof[...]
                    whole = uncentred(iv[spot(b, im, c), cols], num_grad, centre(b, im, q))
                    total = total + colsum(whole * query.astype(F32))
            spread_query = [four(read(fq, b, o)) * mx[...] for o in ones]
            spread_num = [four(read(si, b, o)) * mx[...] for o in ones]
            key = [read(fk, b, o) for o in ones]
            value = [read(vb, b, o) for o in ones]
            score = [(nt(k, s) * cmt[...]).astype(BF16) for k, s in zip(key, spread_query)]
            value_part = [mm(v, s) for v, s in zip(score, spread_num)]
            back = [
                ((nt(v, s) + nt(share, four(read(iv, b, o)) * mx[...])) * cmt[...]).astype(BF16)
                for v, s, o in zip([less(b, o) for o in ones], spread_num, ones)
            ]
            key_part = [mm(v, s) for v, s in zip(back, spread_query)]
            pieces_k, pieces_v = [], []
            for c in range(parts):
                grad = key_part[c] + nt(value[c], states[c][0]) + nt(value[c], states[c][1]) + totals[c]
                pieces_k.append((grad * jnp.minimum(key[c].astype(F32), 1.0)).astype(BF16))
                pieces_v.append((value_part[c] + mm(key[c], states[c][0])).astype(BF16))
            low_k.append(pieces_k)
            low_v.append(pieces_v)
        low_k, low_v = together(low_k), together(low_v)
        g[5, 0:512, :] += tn(first, low_k)
        g[5, 512:1024, :] += tn(first, low_v)
        add(KB, colsum(low_k.astype(F32)))
        add(VB, colsum(low_v.astype(F32)))
        out[image(b, im), :] += nt(low_k, ws[1]) + nt(low_v, ws[2])

    def phase_k(b, c):
        backward.end(b)

        def one(im, c):
            key_side(b, im)
            return c

        lax.fori_loop(0, per, one, 0)
        tick(tick2 + b)
        return c

    clear(CHUNKS - 1, 0)
    lax.fori_loop(0, blocks, phase_k, 0)
    tick3 = tick2 + blocks
    last = times[-1] + 9

    def drain(t, c):
        tick(t)
        return c

    def phase_n(b, c):
        for im in range(per):
            part = image(b, im)
            unit, rate = norm_parts(x[part, :].astype(F32))
            grad = out[part, :]
            add(N1G, colsum(grad * unit))
            add(N1B, colsum(grad))
            x[part, :] = (d2[part, :] + norm_back(grad, unit, rate, row(N1G))).astype(BF16)
        save(ct, lay_hbm, b).wait()
        save(x, ing_hbm, b).start()
        tick(tick3 + b)
        return c

    lax.fori_loop(0, blocks, phase_n, 0)
    lax.fori_loop(tick3 + blocks, last + 1, drain, 0)

    small = [("dp", 1)] + dims

    def swap(i):
        return remote(sb, srx.at[i], s_ss.at[i], s_rs.at[i], peer(small[i]))

    peaks = lax.broadcasted_iota(jnp.int32, (VECS, WIDTH), 0) == PEAK
    for k in range(max(red.steps + 1, len(small) + 1)):
        if k < red.steps:
            chunk4(k)
        if 1 <= k < red.steps + 1:
            chunk5(k - 1)
        if 0 < k <= len(small):
            swap(k - 1).wait()
            came = srx[k - 1]
            sb[...] = jnp.where(peaks, jnp.maximum(sb[...], came), sb[...] + came)
        if k < len(small):
            swap(k).start()
    tail = [
        pltpu.make_async_copy(g.at[4 + i // 2, pl.ds((i % 2) * 512, 512)], h, go_sem.at[4 + i // 2, i % 2])
        for i, h in enumerate((gwo_hbm, gwq_hbm, gwk_hbm, gwv_hbm))
    ]
    for copy in tail:
        copy.start()
    sums_ref[...] = sb[...]
    for b in range(blocks):
        save(x, ing_hbm, b).wait()
    for c in range(4):
        store(c, 0).wait()
        store(c, 1).wait()
    for copy in tail:
        copy.wait()


def red_times(steps):
    gaps = [0, 1, 3, 2] + [1] * (steps - 8) + [1, 1, 2, 1]
    total, times = 0, []
    for gap in gaps:
        total += gap
        times.append(total)
    return times


def per_device(
    seq,
    dp,
    tokens,
    short_counts,
    norm1_gain,
    norm1_bias,
    query_weight,
    query_bias,
    key_weight,
    key_bias,
    value_weight,
    value_bias,
    output_weight,
    output_bias,
    norm2_gain,
    norm2_bias,
    hidden_weight,
    hidden_bias,
    return_weight,
    return_bias,
    cotangent,
):
    images, span, width = tokens.shape
    flat = images * span
    per = 2 if images % 2 == 0 else 1
    blocks, rows = images // per, per * span
    size = 128 if span % 128 == 0 else span
    dims = [("dp", 1 << k) for k in range(1, dp.bit_length() - 1)]
    dims = dims + [("seq", 1 << k) for k in range(seq.bit_length() - 1)]
    turn = (len(dims) - 1) // 3
    orders = [dims[i * turn :] + dims[: i * turn] for i in range(3)]
    red = Reduce(dims, orders)
    limits = jnp.where(jnp.arange(images) < short_counts[0], LEN_SHORT, LEN_LONG).astype(F32)
    small = (norm1_gain, norm1_bias, query_bias, key_bias, value_bias, output_bias, norm2_gain, norm2_bias, return_bias)
    vec = jnp.concatenate(
        [v.astype(F32)[None] for v in small]
        + [hidden_bias.astype(F32).reshape(4, width), jnp.zeros((FIRST_LIMIT - 13, width), F32)]
        + [jnp.broadcast_to(limits[:, None], (images, width))],
        axis=0,
    )
    hbm = pl.BlockSpec(memory_space=pl.ANY)
    vmem = pl.BlockSpec(memory_space=pltpu.VMEM)
    unit = per * 64 + 8
    state = (blocks, unit, QUAD)
    big = lambda kind: pltpu.VMEM((flat, width), kind)
    f32 = lambda *shape: pltpu.VMEM(shape, F32)
    sem = lambda *shape: pltpu.SemaphoreType.DMA(shape)
    scratch = (
        [big(BF16)] * 8
        + [big(F32)] * 2
        + [pltpu.VMEM((4, width, width), BF16)]
        + [pltpu.VMEM((2, width, PART), BF16), pltpu.VMEM((2, PART, width), BF16)]
        + [f32(LANDS + 4, max(CHUNK, red.rows), width)]
        + [f32(VECS, width), f32(len(dims) + 1, VECS, width)]
        + [f32(blocks, 2, unit, QUAD)]
        + [f32(*state)] * 6
        + [f32(blocks, 2, unit, QUAD)] * 2
        + [f32(-(-images // 8) * 8, width)]
        + [pltpu.VMEM((4 * size, QUAD), BF16), pltpu.VMEM((QUAD, QUAD), BF16), f32(QUAD, QUAD)]
        + [f32(size, 4 * size)] * 2
        + [sem(2, blocks), sem(12), sem(blocks), sem(CHUNKS, 2)]
        + [sem(4, red.sems)] * 2
        + [pltpu.SemaphoreType.REGULAR((4, red.frees))]
        + [sem(blocks, 3)] * 4
        + [sem(len(dims) + 1)] * 2
    )
    shape = jax.ShapeDtypeStruct
    square = shape((width, width), F32)
    outs = pl.pallas_call(
        functools.partial(kernel, seq, images, span, red, dims),
        out_shape=(
            shape((flat, width), BF16),
            shape((flat, width), BF16),
            shape(return_weight.shape, F32),
            shape(hidden_weight.shape, F32),
            square,
            square,
            square,
            square,
            shape((VECS, width), F32),
        ),
        in_specs=[hbm, hbm, vmem] + [hbm] * 6,
        out_specs=(hbm,) * 8 + (vmem,),
        scratch_shapes=scratch,
        compiler_params=pltpu.CompilerParams(
            collective_id=0, has_side_effects=True, vmem_limit_bytes=63 * 2**20
        ),
    )(
        tokens.reshape(flat, width),
        cotangent.reshape(flat, width),
        vec,
        query_weight,
        key_weight,
        value_weight,
        output_weight,
        hidden_weight,
        return_weight,
    )
    lay, ing, gw2, gw1, gwo, gwq, gwk, gwv, sums = outs
    peak = jnp.max(sums[PEAK]) / (span * seq * (width // HEADS))
    return (
        lay.reshape(images, span, width),
        ing.reshape(images, span, width),
        peak,
        sums[N1G],
        sums[N1B],
        gwq,
        sums[QB],
        gwk,
        sums[KB],
        gwv,
        sums[VB],
        gwo,
        sums[OB],
        sums[N2G],
        sums[N2B],
        gw1,
        sums[HB : HB + 4].reshape(-1),
        gw2,
        sums[RB],
    )


def solution(mesh):
    split = P("dp", "seq", None)
    return jax.shard_map(
        functools.partial(per_device, mesh.shape["seq"], mesh.shape["dp"]),
        mesh=mesh,
        in_specs=(split, P("dp")) + (P(),) * 16 + (split,),
        out_specs=(split, split) + (P(),) * 17,
        check_vma=False,
    )
```

time: 917 us -> 286 us (0.31); the launches traced: 906 us -> 285 us
  matrix products: 322 us -> 0 us
  Pallas kernels: 0 us -> 255 us
  waiting for transfers between devices: 224 us -> 0 us
  blocking collectives: 170 us -> 0 us
  local copies, waits for them, and re-layouts: 113 us -> 19.3 us
  other arithmetic: 60.6 us -> 8.48 us
  between operations: 16.4 us -> 3.12 us
    dot_general x32 -> x0, matrix products: 322 us -> none  [the longest x6 78.6 us: matmul(): return jnp.dot(left, right, preferred_element_type=jnp.float32)]
    pallas_call x0 -> x1, Pallas kernels: none -> 255 us  [per_device(): pl.pallas_call(functools.partial(kernel, seq, images, span, red, dims), o...]
    psum x1 -> x0, waiting for transfers between devices: 114 us -> none  [per_device(): summed = lax.psum(attn_grads + ffn_grads, ('dp', 'seq'))]
    all_gather x2 -> x0, waiting for transfers between devices: 109 us -> none  [entering(): gathered = jax.tree.map(lambda a: lax.all_gather(a, axis), part)]
    all_gather x2 -> x0, blocking collectives: 85.7 us -> none  [entering(): gathered = jax.tree.map(lambda a: lax.all_gather(a, axis), part)]
    reshape x11 -> x1, local copies, waits for them, and re-layouts: 83.8 us -> 0.7 us  [per_device(): hidden_bias.astype(F32).reshape(4, width)]
    psum x1 -> x0, blocking collectives: 45 us -> none  [per_device(): summed = lax.psum(attn_grads + ffn_grads, ('dp', 'seq'))]
    pmax x1 -> x0, blocking collectives: 38.8 us -> none  [per_device(): den_peak = lax.pmax(local_peak, ('dp', 'seq'))]
  transfers between devices with their start and end apart: 3 -> 0, of which waited for: 3 -> 0; matrix products, arithmetic and copies ran while one was open for 25% -> 0% of each run, Pallas kernels for 0% -> 0%
where the time goes in v1:
time: 286 us; the launch traced here: 285 us
  Pallas kernels  255 us (89%)
  local copies, waits for them, and re-layouts  19.3 us (7%)
  other arithmetic  8.48 us (3%)
  between operations  3.12 us (1%)
    pallas_call x1, Pallas kernels, per_device(): pl.pallas_call(functools.partial(kernel, seq, images, span, red, dims), o...  255 us
    unnamed x24, local copies, waits for them, and re-layouts  16.7 us
    broadcast_in_dim x9, other arithmetic, per_device(): v.astype(F32)[None]  6.13 us

profile of v1, /device:TPU:0, one launch (start us, length us, event | category | flops | bytes accessed | tf_op | source)
XLA Modules:
  0.0 285.4 jit_solution(11515754872043812177)
XLA Ops:
  1.3 0.7 broadcast_in_dim.93
  2.0 0.7 broadcast_in_dim.94
  2.7 0.7 broadcast_in_dim.95
  3.4 0.7 broadcast_in_dim.96
  4.0 0.7 broadcast_in_dim.97
  4.7 0.7 broadcast_in_dim.98
  5.4 0.7 broadcast_in_dim.99
  6.1 0.7 broadcast_in_dim.100
  6.8 0.7 broadcast_in_dim.101
  7.4 0.7 reshape.82
  8.1 0.1 broadcast_in_dim.92
  8.2 1.9 concatenate.3.vec
  10.1 254.5 %shard_map.330 = (bf16[2304,512]{1,0:T(8,128)(2,1)}, bf16[2304,512]{1,0:T(8,128)(2,1)}, f32[2048,512]{1,0:T(8,128)}, f32[512,2048]{1,0:T(8,128)}, f32[512,512]{1...) custom-call(bf16[2304,512]{1,0:T(8,128)(2,1)} %bitcast.29, ...), custom_call_target="tpu_custom_call" | custom-call | tf_op jit(solution)/shard_map/pallas_call | solution.py:907
  264.6 0.7 slice_bitcast_fusion
  265.3 2.3 fusion.1
  268.3 0.6 copy.38
  268.9 0.0 copy-start.2
  268.9 3.5 %copy.48 = bf16[6,384,512]{2,1,0:T(8,128)(2,1)} copy(bf16[6,384,512]{2,1,0:T(8,128)(2,1)} %bitcast.28) | data formatting | bytes 4718592
  272.5 0.0 copy-done.2
  272.5 0.0 copy-start.6
  272.5 0.0 copy-start.5
  272.5 1.4 copy.49
  273.9 0.5 copy-done.6
  274.4 0.0 copy-start.4
  274.4 0.0 copy-start.3
  274.4 1.0 copy.50
  275.4 0.0 copy-done.5
  275.4 0.0 copy-start.1
  275.4 1.0 copy.51
  276.4 0.0 copy-done.4
  276.4 1.0 copy.52
  277.3 0.0 copy-done.3
  277.3 1.0 copy.53
  278.3 0.3 copy-done.1
  278.6 0.0 copy-start
  278.6 2.1 copy.54
  280.7 1.6 copy-done
  282.3 2.0 copy.55
  (2 shorter events, 0.0 us)
Async XLA Ops:
  268.9 3.5 %copy-start.2 = (bf16[2304,512]{1,0:T(8,128)(2,1)S(1)}, bf16[2304,512]{1,0:T(8,128)(2,1)}, u32[]{:S(2)}) copy-start(bf16[2304,512]{1,0:T(8,128)(2,1)} %get-tuple-element.29) | copy-start | bytes 7077892
  272.5 2.0 copy-start.6
  272.5 2.9 %copy-start.5 = (f32[512,512]{1,0:T(8,128)S(1)}, f32[512,512]{1,0:T(8,128)}, u32[]{:S(2)}) copy-start(f32[512,512]{1,0:T(8,128)} %get-tuple-element.73) | copy-start | bytes 3145732
  274.4 2.0 copy-start.4
  274.4 2.9 %copy-start.3 = (f32[512,512]{1,0:T(8,128)S(1)}, f32[512,512]{1,0:T(8,128)}, u32[]{:S(2)}) copy-start(f32[512,512]{1,0:T(8,128)} %get-tuple-element.77) | copy-start | bytes 3145732
  275.4 3.2 %copy-start.1 = (f32[512,2048]{1,0:T(8,128)S(1)}, f32[512,2048]{1,0:T(8,128)}, u32[]{:S(2)}) copy-start(f32[512,2048]{1,0:T(8,128)} %get-tuple-element.81) | copy-start | bytes 12582916
  278.6 3.7 %copy-start = (f32[2048,512]{1,0:T(8,128)S(1)}, f32[2048,512]{1,0:T(8,128)}, u32[]{:S(2)}) copy-start(f32[2048,512]{1,0:T(8,128)} %get-tuple-element.83) | copy-start | bytes 12582916

commit v2 on v1

v2 whole, which is shorter than its diff:
```python
import functools

import jax
import jax.numpy as jnp
from jax import lax
from jax.experimental import pallas as pl
from jax.experimental.pallas import tpu as pltpu
from jax.sharding import PartitionSpec as P

HEADS = 8
LEN_LONG = 3072
LEN_SHORT = 784
EPSILON = 1e-05
F32, BF16 = jnp.float32, jnp.bfloat16
MESH = pl.DeviceIdType.MESH

WIDTH = 512
PART = 512
QUAD = 256
DEPTH = 64
HALVINGS = 3
CHUNK = 1024
CHUNKS = 6
LANDS = 5
SHARES = (4, 3, 1)
VECS = 16


def mm(a, b):
    return lax.dot_general(a, b, (((1,), (0,)), ((), ())), preferred_element_type=F32)


def nt(a, b):
    return lax.dot_general(a, b, (((1,), (1,)), ((), ())), preferred_element_type=F32)


def tn(a, b):
    return lax.dot_general(a, b, (((0,), (0,)), ((), ())), preferred_element_type=F32)


def colsum(v):
    return jnp.sum(v, axis=0, keepdims=True)


def bit(index, step):
    return lax.rem(lax.div(index, step), 2)


def aligned(v, m=8):
    return v if isinstance(v, int) else pl.multiple_of(v, m)


def coord(dim):
    return bit(lax.axis_index(dim[0]), dim[1])


def peer(dim):
    axis, step = dim
    d, s = lax.axis_index("dp"), lax.axis_index("seq")
    if axis == "dp":
        return (d + step * (1 - 2 * bit(d, step)), s)
    return (d, s + step * (1 - 2 * bit(s, step)))


def remote(src, dst, send, recv, device):
    return pltpu.make_async_remote_copy(
        src_ref=src, dst_ref=dst, send_sem=send, recv_sem=recv, device_id=device, device_id_type=MESH
    )


class Reduce:
    def __init__(self, dims, orders):
        self.core, self.orders = ("dp", 1), orders
        self.half = CHUNK // 2
        unit = self.half // sum(SHARES)
        self.sizes = [unit * s for s in SHARES]
        self.starts = [sum(self.sizes[:i]) for i in range(len(SHARES))]
        self.whole = len(dims) - HALVINGS
        self.between = 2 * HALVINGS + self.whole
        self.steps = self.between + 3
        self.sems = 2 + len(SHARES) * self.between
        self.frees = 1 + len(SHARES) * (HALVINGS + self.whole)
        self.turn = HALVINGS + self.whole + 1
        self.bases = [self.half]
        for p in range(len(SHARES)):
            self.bases.append(self.bases[-1] + self.offset(p, HALVINGS + self.whole))
        self.rows = self.bases[-1]

    def offset(self, p, k):
        n = self.sizes[p]
        over = max(k - HALVINGS, 0)
        return n - (n >> min(k, HALVINGS)) + over * (n >> HALVINGS)

    def piece(self, p, k):
        at = coord(self.core) * self.half + self.starts[p]
        for i in range(k):
            at = at + coord(self.orders[p][i]) * (self.sizes[p] >> (i + 1))
        return at

    def copies(self, g, r, ss, rs, stage):
        half = self.half
        if stage in (0, self.steps - 2):
            c = coord(self.core)
            mine, other = aligned(c * half), aligned((1 - c) * half)
            if stage == 0:
                dst = r.at[pl.ds(0, half)]
                cp = remote(g.at[pl.ds(other, half)], dst, ss.at[0], rs.at[0], peer(self.core))
                return [(cp, mine, 0, half, 0, peer(self.core))]
            part = g.at[pl.ds(mine, half)]
            cp = remote(part, part, ss.at[1], rs.at[1], peer(self.core))
            return [(cp, None, None, half, None, peer(self.core))]
        out = []
        k = stage - 1
        for p, order in enumerate(self.orders):
            n = self.sizes[p]
            sem = 2 + p * self.between + k
            land = self.bases[p] + self.offset(p, k)
            free = 1 + p * (HALVINGS + self.whole) + k
            if k < HALVINGS:
                m, dim, base = n >> (k + 1), order[k], self.piece(p, k)
                c = coord(dim)
                src = g.at[pl.ds(aligned(base + (1 - c) * m), m)]
                dst, to = r.at[pl.ds(land, m)], aligned(base + c * m)
            elif k < HALVINGS + self.whole:
                m, dim, to = n >> HALVINGS, order[k], aligned(self.piece(p, HALVINGS))
                src, dst = g.at[pl.ds(to, m)], r.at[pl.ds(land, m)]
            else:
                i = self.between - 1 - k
                free = None
                m, dim, to, land = n >> (i + 1), order[i], None, None
                src = dst = g.at[pl.ds(aligned(self.piece(p, i + 1)), m)]
            cp = remote(src, dst, ss.at[sem], rs.at[sem], peer(dim))
            out.append((cp, to, land, m, free, peer(dim)))
        return out

    def step(self, g, r, ss, rs, fs, k):
        if k > 0:
            for cp, to, land, m, free, device in self.copies(g, r, ss, rs, k - 1):
                cp.wait()
                if to is not None:
                    slab = next(s for s in (64, 48, 32, 24, 16, 8) if m % s == 0)

                    def one(i, c, to=to, land=land, slab=slab):
                        a = pl.ds(pl.multiple_of(to + i * slab, 8), slab)
                        g[a, :] += r[pl.ds(pl.multiple_of(land + i * slab, 8), slab), :]
                        return c

                    lax.fori_loop(0, m // slab, one, 0)
                    pl.semaphore_signal(fs.at[free], inc=1, device_id=device, device_id_type=MESH)
        for n in range(HALVINGS + 1 if k == self.turn else 0):
            self.freed(fs, n)
        for n in range(HALVINGS + 1, self.turn if k == self.turn + 1 else 0):
            self.freed(fs, n)
        if k < self.steps - 1:
            for cp, *_ in self.copies(g, r, ss, rs, k):
                cp.start()

    def freed(self, fs, stage):
        if stage == 0:
            pl.semaphore_wait(fs.at[0], 1)
        else:
            for p in range(len(SHARES)):
                pl.semaphore_wait(fs.at[1 + p * (HALVINGS + self.whole) + stage - 1], 1)


class Scan:
    def __init__(self, seq, back, own, rx1, rxp, txp, tx2, rx2, prior, ss, rs):
        self.hops = seq // 2
        place = lax.axis_index("seq")
        self.dp, self.place = lax.axis_index("dp"), place
        lo, hi = lax.rem(place, 2), lax.div(place, 2)
        self.partner = (self.dp, place + 1 - 2 * lo)
        self.next = (self.dp, place - 2 if back else place + 2)
        self.lo = 1 - lo if back else lo
        self.hi = self.hops - 1 - hi if back else hi
        self.own, self.rx1, self.rxp, self.txp = own, rx1, rxp, txp
        self.tx2, self.rx2, self.prior, self.ss, self.rs = tx2, rx2, prior, ss, rs

    def first(self, i):
        src = self.own.at[i, 1 - self.lo]
        return remote(src, self.rx1.at[i], self.ss.at[i, 0], self.rs.at[i, 0], self.partner)

    def chain(self, i):
        return remote(
            self.txp.at[i], self.rxp.at[i], self.ss.at[i, 1], self.rs.at[i, 1], self.next
        )

    def last(self, i):
        return remote(
            self.tx2.at[i], self.rx2.at[i], self.ss.at[i, 2], self.rs.at[i, 2], self.partner
        )

    def begin(self, i):
        self.first(i).start()

    def hop(self, i):
        @pl.when(self.hi == 0)
        def _():
            self.rxp[i] = jnp.zeros_like(self.rxp[i])

        self.first(i).wait()
        mine = self.own[i, self.lo]
        other = self.rx1[i]

        @pl.when(self.hi > 0)
        def _():
            self.chain(i).wait_recv()

        came = self.rxp[i]

        @pl.when(self.hi < self.hops - 1)
        def _():
            self.txp[i] = came + mine + other
            self.chain(i).start()

        upper = self.lo.astype(F32)
        self.tx2[i] = came + (1.0 - upper) * mine
        self.last(i).start()
        self.prior[i, self.lo] = came + upper * other

    def end(self, i):
        self.last(i).wait()

        @pl.when(self.hi < self.hops - 1)
        def _():
            self.chain(i).wait_send()

        self.prior[i, 1 - self.lo] = self.rx2[i]


def norm_parts(v):
    centre = v - jnp.mean(v, axis=-1, keepdims=True)
    rate = lax.rsqrt(jnp.mean(centre * centre, axis=-1, keepdims=True) + EPSILON)
    return centre * rate, rate


def norm_back(grad, unit, rate, gain):
    inner = grad * gain
    shift = jnp.mean(inner, axis=-1, keepdims=True)
    scale = jnp.mean(inner * unit, axis=-1, keepdims=True)
    return rate * (inner - shift - unit * scale)


def feature(v):
    return jnp.where(v > 0, v + 1.0, jnp.exp(jnp.minimum(v, 0.0)))


def normal_parts(u):
    e = jnp.exp(-0.5 * u * u)
    t = 1.0 / (1.0 + 0.3275911 * 0.7071067811865476 * jnp.abs(u))
    poly = 1.421413741 + t * (-1.453152027 + t * 1.061405429)
    poly = t * (0.254829592 + t * (-0.284496736 + t * poly))
    tail = 0.5 * poly * e
    return jnp.where(u > 0, 1.0 - tail, tail), e * 0.3989422804014327


def split(v):
    high = v.astype(BF16)
    return high, (v - high.astype(F32)).astype(BF16)


def four(v):
    return jnp.concatenate([v] * 4, axis=0)


def fold(v):
    return v[0:64] + v[64:128] + v[128:192] + v[192:256]


def spread(v):
    inside = lax.broadcasted_iota(jnp.int32, (v.shape[0], 128), 1) < DEPTH
    out = []
    for t in range(2):
        tile = v[:, t * 128 : (t + 1) * 128]
        turned = pltpu.roll(tile, DEPTH, 1)
        out += [jnp.where(inside, tile, turned), jnp.where(inside, turned, tile)]
    return out


N1G, N1B, QB, KB, VB, OB, N2G, N2B, RB, HB = range(10)
PEAK = 13


def kernel(
    seq,
    images,
    span,
    red,
    dims,
    tok_hbm,
    cot_hbm,
    short_ref,
    vec_refs,
    wq_hbm,
    wk_hbm,
    wv_hbm,
    wo_hbm,
    w1_hbm,
    w2_hbm,
    lay_hbm,
    ing_hbm,
    gw2_hbm,
    gw1_hbm,
    gwo_hbm,
    gwq_hbm,
    gwk_hbm,
    gwv_hbm,
    sums_ref,
    x,
    ct,
    fq,
    fk,
    vb,
    at,
    iv,
    si,
    out,
    d2,
    ws,
    w1,
    w2,
    g,
    vec,
    sb,
    srx,
    own,
    rx1,
    f_rxp,
    b_rxp,
    txp,
    tx2,
    rx2,
    f_prior,
    b_prior,
    mu,
    dgt,
    gsum,
    mx,
    bo,
    bof,
    cm,
    cmt,
    in_sem,
    w_sem,
    out_sem,
    go_sem,
    red_ss,
    red_rs,
    red_fs,
    f_ss,
    f_rs,
    b_ss,
    b_rs,
    s_ss,
    s_rs,
):
    per = 2 if images % 2 == 0 else 1
    blocks = images // per
    rows = per * span
    size = 128 if span % 128 == 0 else span
    parts = span // size
    place = lax.axis_index("seq")
    small = [("dp", 1)] + dims

    step_s = images
    step_b = step_s + images
    step_f = step_b + 2 * blocks
    step_g = step_f + 2 * blocks
    step_q = step_g + 2 * blocks
    step_k = step_q + images
    step_n = step_k + images
    step_d = step_n + blocks
    times = red_times(red.steps)
    starts = [step_f - 1, step_f + blocks - 1, step_g - 1, step_q - 2]
    starts.append(max(step_k - 1, starts[1] + times[red.turn + 1]))
    starts.append(max(step_n - 1, starts[2] + times[red.turn + 1]))
    total_steps = max(starts[-1] + times[-1], step_d + len(small)) + 1

    def image(i):
        return pl.ds(pl.multiple_of(i * span, 16), span)

    def block(b):
        return pl.ds(pl.multiple_of(b * rows, 16), rows)

    def spot(i, c):
        return pl.ds(pl.multiple_of(i * span + c * size, 16), size)

    def fetch(hbm, ref, sem, i):
        return pltpu.make_async_copy(hbm.at[image(i)], ref.at[image(i)], sem.at[i])

    def save(ref, hbm, b):
        return pltpu.make_async_copy(ref.at[block(b)], hbm.at[block(b)], out_sem.at[b])

    fetch(tok_hbm, x, in_sem.at[0], 0).start()
    loads = [
        pltpu.make_async_copy(h, ws.at[i], w_sem.at[i])
        for i, h in enumerate((wq_hbm, wk_hbm, wv_hbm, wo_hbm))
    ]
    for load in loads[:3]:
        load.start()
    for i in range(1, images):
        fetch(tok_hbm, x, in_sem.at[0], i).start()
    loads[3].start()

    def weights(j):
        cols = pl.ds(j * PART, PART)
        return (
            pltpu.make_async_copy(w1_hbm.at[:, cols], w1.at[j % 2], w_sem.at[4 + j]),
            pltpu.make_async_copy(w2_hbm.at[cols, :], w2.at[j % 2], w_sem.at[8 + j]),
        )

    def fill(j):
        for load in weights(j):
            load.start()

    def filled(j):
        for load in weights(j):
            load.wait()

    fill(0)
    fill(1)
    for i in range(images):
        fetch(cot_hbm, ct, in_sem.at[1], i).start()

    barrier = pltpu.get_barrier_semaphore()
    chain = [(lax.axis_index("dp"), lax.rem(place + d, seq)) for d in (2, seq - 2)]
    friends = [peer(d) for d in small] + chain
    for friend in friends:
        pl.semaphore_signal(barrier, inc=1, device_id=friend, device_id_type=MESH)

    for i, ref in enumerate(vec_refs):
        vec[i : i + ref.shape[0] // WIDTH, :] = ref[...].astype(F32).reshape(-1, WIDTH)

    def iota(shape, axis):
        return lax.broadcasted_iota(jnp.int32, shape, axis)

    tile = (QUAD, QUAD)
    bof[...] = jnp.where(iota(tile, 0) // DEPTH == iota(tile, 1) // DEPTH, 1.0, 0.0)
    bo[...] = bof[...].astype(BF16)
    tall = (4 * size, QUAD)
    mx[...] = jnp.where(iota(tall, 0) // size == iota(tall, 1) // DEPTH, 1.0, 0.0).astype(BF16)
    wide = (size, 4 * size)
    cm[...] = jnp.where(iota(wide, 1) % size <= iota(wide, 0), 1.0, 0.0)
    cmt[...] = jnp.where(iota(wide, 1) % size >= iota(wide, 0), 1.0, 0.0)
    sb[...] = jnp.zeros_like(sb)

    def clear(c, ignored):
        def inner(k, ignored):
            g[c, pl.ds(pl.multiple_of(k * 64, 8), 64), :] = jnp.zeros((64, WIDTH), F32)
            return ignored

        return lax.fori_loop(0, CHUNK // 64, inner, ignored)

    def row(i):
        return vec[i : i + 1, :]

    def add(i, v):
        sb[i : i + 1, :] += v

    def limit(i):
        return jnp.where(i < short_ref[0], LEN_SHORT, LEN_LONG)

    def positions(start, count, width):
        return iota((count, width), 0) + (place * span + start)

    forward = Scan(seq, False, own, rx1, f_rxp, txp, tx2, rx2, f_prior, f_ss, f_rs)
    backward = Scan(seq, True, own, rx1, b_rxp, txp, tx2, rx2, b_prior, b_ss, b_rs)
    halves = [slice(q * QUAD, (q + 1) * QUAD) for q in range(2)]
    cells = [(q, c) for q in range(2) for c in range(parts)]

    def read(ref, i, q, c):
        return ref[spot(i, c), halves[q]]

    def together(pieces):
        rows_of = [jnp.concatenate(pieces[q * parts : (q + 1) * parts], axis=0) for q in range(2)]
        return jnp.concatenate(rows_of, axis=1)

    def put(i, q, state, total):
        own[i, q, 0:64, :] = fold(state)
        own[i, q, 64:65, :] = total

    def known(ref, i, q):
        return four(ref[i, q, 0:64, :]) * bof[...], ref[i, q, 64:65, :]

    def centre(i, q):
        return mu[pl.ds(i, 1), halves[q]]

    def head_sums(v):
        high, low = split(v)
        return mm(high, bo[...]) + mm(low, bo[...])

    def project(i):
        fetch(tok_hbm, x, in_sem.at[0], i).wait()

        @pl.when(i == 0)
        def _():
            for load in loads[:3]:
                load.wait()

        part = image(i)
        unit, _ = norm_parts(x[part, :].astype(F32))
        first = (unit * row(N1G) + row(N1B)).astype(BF16)
        key = feature(mm(first, ws[1]) + row(KB))
        inside = positions(0, span, WIDTH) < limit(i)
        key = jnp.where(inside, key, 0.0).astype(BF16)
        fk[part, :] = key
        value = (mm(first, ws[2]) + row(VB)).astype(BF16)
        vb[part, :] = value
        total = colsum(key.astype(F32))
        for q, cols in enumerate(halves):
            put(i, q, tn(key[:, cols], value[:, cols]) * bof[...], total[:, cols])
        fq[part, :] = feature(mm(first, ws[0]) + row(QB)).astype(BF16)

        @pl.when(i == 0)
        def _():
            pl.semaphore_wait(barrier, len(friends))

        forward.begin(i)

    def within(i):
        query = [read(fq, i, *o) for o in cells]
        score = [(nt(u, four(read(fk, i, *o)) * mx[...]) * cm[...]).astype(BF16) for u, o in zip(query, cells)]
        num = [mm(v, four(read(vb, i, *o)) * mx[...]) for v, o in zip(score, cells)]
        den = [mm(v, mx[...]) for v in score]
        for n, d, (q, c) in zip(num, den, cells):
            out[spot(i, c), halves[q]] = n
            d2[spot(i, c), halves[q]] = d

        @pl.when(i < LANDS)
        def _():
            clear(i, 0)

    def entering(i, q):
        state, total = known(f_prior, i, q)
        states, totals = [], []
        for c in range(parts):
            states.append(split(state))
            totals.append(total)
            if c < parts - 1:
                key = read(fk, i, q, c)
                state = state + tn(key, read(vb, i, q, c)) * bof[...]
                total = total + colsum(key.astype(F32))
        return states, totals

    def attend(i):
        forward.end(i)
        for q, cols in enumerate(halves):
            state, total = f_prior[i, q, 0:64, :], f_prior[i, q, 64:65, :]
            count = total + own[i, q, 64:65, :]
            count = head_sums(jnp.broadcast_to(count, (8, QUAD)))[0:1]
            off = colsum(state + own[i, q, 0:64, :]) / count
            mu[pl.ds(i, 1), cols] = off
        ahead = [entering(i, q) for q in range(2)]
        inside = positions(0, span, QUAD) < limit(i)
        for q, c in cells:
            at_spot = (spot(i, c), halves[q])
            query, off = fq[at_spot], centre(i, q)
            high, low = ahead[q][0][c]
            n = out[at_spot] + mm(query, high) + mm(query, low)
            d = d2[at_spot] + head_sums(query.astype(F32) * ahead[q][1][c])
            inverse = 1.0 / d
            at[at_spot] = (n * inverse - off).astype(BF16)
            iv[at_spot] = inverse.astype(BF16)
            peak = jnp.max(jnp.where(inside[c * size : (c + 1) * size], d, 0.0), axis=0, keepdims=True)
            sb[PEAK : PEAK + 1, halves[q]] = jnp.maximum(sb[PEAK : PEAK + 1, halves[q]], peak)
        part = image(i)
        mid = x[part, :].astype(F32) + mm(attended(i), ws[3]) + row(OB)
        unit, _ = norm_parts(mid)
        si[part, :] = (unit * row(N2G) + row(N2B)).astype(BF16)
        out[part, :] = mid + row(RB)
        d2[part, :] = jnp.zeros((span, WIDTH), F32)
        fetch(cot_hbm, ct, in_sem.at[1], i).wait()
        add(RB, colsum(ct[part, :].astype(F32)))

    def attended(i):
        return (at[image(i), :].astype(F32) + mu[pl.ds(i, 1), :]).astype(BF16)

    def feed(j, b):
        normed, grad = si[block(b), :], ct[block(b), :]
        up, down = w1[lax.rem(j, 2)], w2[lax.rem(j, 2)]
        act, pre = [], []
        for im in range(per):
            part = slice(im * span, (im + 1) * span)
            hidden = mm(normed[part], up) + vec[pl.ds(HB + j, 1), :]
            back = nt(grad[part], down)
            cdf, pdf = normal_parts(hidden)
            act.append((hidden * cdf).astype(BF16))
            pre.append((back * (cdf + hidden * pdf)).astype(BF16))
            out[image(b * per + im), :] += mm(act[im], down)
            d2[image(b * per + im), :] += nt(pre[im], up)
        act, pre = jnp.concatenate(act, axis=0), jnp.concatenate(pre, axis=0)
        g[j, 0:512, :] += tn(act, grad)
        g[j, 512:1024, :] += tn(normed, pre)
        sb[pl.ds(HB + j, 1), :] += colsum(pre.astype(F32))

    def norm_two(i):
        part = image(i)
        attn = attended(i)
        unit, rate = norm_parts(x[part, :].astype(F32) + mm(attn, ws[3]) + row(OB))
        grad = d2[part, :]
        add(N2G, colsum(grad * unit))
        add(N2B, colsum(grad))
        residual = ct[part, :].astype(F32) + norm_back(grad, unit, rate, row(N2G))
        d2[part, :] = residual
        ct[part, :] = out[part, :].astype(BF16)
        low = residual.astype(BF16)
        mixed_grad = nt(low, ws[3])
        inverse = iv[part, :].astype(F32)
        num_grad = (mixed_grad * inverse).astype(BF16)
        si[part, :] = num_grad
        inner = num_grad.astype(F32) * (at[part, :].astype(F32) + mu[pl.ds(i, 1), :])
        den_grad = jnp.concatenate([-head_sums(inner[:, cols]) for cols in halves], axis=1)
        high, low_part = split(den_grad)
        iv[part, :] = high
        at[part, :] = low_part
        query = fq[part, :]
        totals = den_grad * query.astype(F32)
        totals = [colsum(totals[c * size : (c + 1) * size]) for c in range(parts)]
        for c in range(1, parts):
            gsum[pl.ds(i * parts + c, 1), :] = totals[c]
        total = functools.reduce(lambda a, b: a + b, totals)
        for q, cols in enumerate(halves):
            put(i, q, tn(query[:, cols], num_grad[:, cols]) * bof[...], total[:, cols])
        backward.begin(i)
        pick = jnp.where(iota((8, WIDTH), 1) == iota((8, WIDTH), 0) * DEPTH, 1.0, 0.0).astype(BF16)
        dgt[i] = nt(pick, high) + nt(pick, low_part)
        g[4, 0:512, :] += tn(attn, low)
        add(OB, colsum(low.astype(F32)))

    def query_side(i):
        unit, _ = norm_parts(x[image(i), :].astype(F32))
        first = (unit * row(N1G) + row(N1B)).astype(BF16)
        ahead = [entering(i, q) for q in range(2)]
        num_grad = [read(si, i, *o) for o in cells]
        den_grad = [read(iv, i, *o).astype(F32) + read(at, i, *o).astype(F32) for o in cells]
        at[image(i), :] = first
        back = [nt(n, four(read(vb, i, *o)) * mx[...]) for n, o in zip(num_grad, cells)]
        back = [
            ((v + jnp.concatenate(spread_rows(d), axis=1)) * cm[...]).astype(BF16)
            for v, d in zip(back, den_grad)
        ]
        side = [mm(v, four(read(fk, i, *o)) * mx[...]) for v, o in zip(back, cells)]
        low = []
        for u, n, d, (q, c) in zip(side, num_grad, den_grad, cells):
            high, part = ahead[q][0][c]
            grad = u + nt(n, high) + nt(n, part) + d * ahead[q][1][c]
            low.append((grad * jnp.minimum(read(fq, i, q, c).astype(F32), 1.0)).astype(BF16))
        low = together(low)
        g[4, 512:1024, :] += tn(first, low)
        add(QB, colsum(low.astype(F32)))
        out[image(i), :] = nt(low, ws[0])

    def spread_rows(v):
        return [u[:, :size] for u in spread(v)]

    def key_side(i):
        backward.end(i)
        first = at[image(i), :]
        low_k, low_v = [], []
        for q in range(2):
            state, total = known(b_prior, i, q)
            states, totals = [], []
            for c in reversed(range(parts)):
                states.insert(0, split(state))
                totals.insert(0, total)
                if c > 0:
                    state = state + tn(read(fq, i, q, c), read(si, i, q, c)) * bof[...]
                    total = total + gsum[pl.ds(i * parts + c, 1), halves[q]]
            wide_query = [four(read(fq, i, q, c)) * mx[...] for c in range(parts)]
            wide_num = [four(read(si, i, q, c)) * mx[...] for c in range(parts)]
            key = [read(fk, i, q, c) for c in range(parts)]
            value = [read(vb, i, q, c) for c in range(parts)]
            score = [(nt(k, u) * cmt[...]).astype(BF16) for k, u in zip(key, wide_query)]
            value_part = [mm(v, u) for v, u in zip(score, wide_num)]
            back = []
            for c in range(parts):
                line = [dgt[i, 4 * q + h : 4 * q + h + 1, c * size : (c + 1) * size] for h in range(4)]
                line = jnp.concatenate(line, axis=1)
                back.append(((nt(value[c], wide_num[c]) + line) * cmt[...]).astype(BF16))
            key_part = [mm(v, u) for v, u in zip(back, wide_query)]
            for c in range(parts):
                (high, part), total = states[c], totals[c]
                grad = key_part[c] + nt(value[c], high) + nt(value[c], part) + total
                low_k.append((grad * jnp.minimum(key[c].astype(F32), 1.0)).astype(BF16))
                low_v.append((value_part[c] + mm(key[c], high)).astype(BF16))
        low_k, low_v = together(low_k), together(low_v)
        g[5, 0:512, :] += tn(first, low_k)
        g[5, 512:1024, :] += tn(first, low_v)
        add(KB, colsum(low_k.astype(F32)))
        add(VB, colsum(low_v.astype(F32)))
        out[image(i), :] += nt(low_k, ws[1]) + nt(low_v, ws[2])

    def norm_one(i):
        part = image(i)
        unit, rate = norm_parts(x[part, :].astype(F32))
        grad = out[part, :]
        add(N1G, colsum(grad * unit))
        add(N1B, colsum(grad))
        x[part, :] = (d2[part, :] + norm_back(grad, unit, rate, row(N1G))).astype(BF16)

    def over(body):
        def run(b):
            def one(im, ignored):
                body(b * per + im)
                return ignored

            lax.fori_loop(0, per, one, 0)

        return run

    def results(c):
        cols = pl.ds(pl.multiple_of(c * PART, PART), PART)
        two = [
            (c < 4, gw2_hbm.at[cols, :], gw1_hbm.at[:, cols]),
            (c == 4, gwo_hbm, gwq_hbm),
            (c == 5, gwk_hbm, gwv_hbm),
        ]
        upper, lower = g.at[c, pl.ds(0, 512)], g.at[c, pl.ds(512, 512)]
        return [
            (when, (pltpu.make_async_copy(upper, a, go_sem.at[c, 0]), pltpu.make_async_copy(lower, b, go_sem.at[c, 1])))
            for when, a, b in two
        ]

    def due(u):
        for k in reversed(range(red.steps)):
            c = -1
            for n, start in enumerate(starts):
                c = jnp.where(u == start + times[k], n, c)

            @pl.when(c >= 0)
            def _(k=k, c=c):
                land = LANDS + c - jnp.where(c >= 4, 3, 0)
                red.step(g.at[c], g.at[land], red_ss.at[c], red_rs.at[c], red_fs.at[c], k)
                if k == red.steps - 1:
                    for when, copies in results(c):

                        @pl.when(when)
                        def _(copies=copies):
                            for copy in copies:
                                copy.start()

    def swap(k):
        return remote(sb, srx.at[k], s_ss.at[k], s_rs.at[k], peer(small[k]))

    def swaps(u):
        peaks = iota((VECS, WIDTH), 0) == PEAK
        for k in range(len(small) + 1):

            @pl.when(u == step_d + k)
            def _(k=k):
                if k > 0:
                    swap(k - 1).wait()
                    came = srx[k - 1]
                    sb[...] = jnp.where(peaks, jnp.maximum(sb[...], came), sb[...] + came)
                if k < len(small):
                    swap(k).start()

    def hops(scan, start, stop):
        def one(i, ignored):
            scan.hop(i)
            return ignored

        lax.fori_loop(start, stop, one, 0)

    def ready(scan, begun, now, least):
        count = jnp.maximum(0, least)
        for i in range(images):
            arrived = begun[i] + 42 + 39 * scan.hi <= now
            count = jnp.maximum(count, jnp.where(arrived, i + 1, 0))
        return count

    opened = [13 * (i + 1) + 3 * i for i in range(images)]
    turned = [56 + 78 * (i // per) + 22 * (i % per) for i in range(images)]

    def forward_by(u):
        v = u - step_b
        late = 13 * step_b + 39 * v
        now = jnp.where(u < step_b, 13 * (u + 1), late)
        least = jnp.where(u < step_b, 0, per * (1 + lax.div(v, 2)))
        return ready(forward, opened, now, jnp.clip(least, 0, images))

    def hops_forward(u):
        hops(forward, jnp.where(u == 0, 0, forward_by(u - 1)), forward_by(u))

    def backward_by(u):
        v, w, y = u - step_g, u - step_q, u - step_k
        in_g = 78 * lax.div(v, 2) + jnp.where(lax.rem(v, 2) == 0, 34, 78)
        now = jnp.where(u < step_q, in_g, jnp.where(u < step_k, 78 * blocks + 24 * (w + 1), 78 * blocks + 24 * images + 33 * (y + 1)))
        least = jnp.clip(jnp.where(u < step_k - 1, 0, y + 2), 0, images)
        return ready(backward, turned, now - 20, least)

    def hops_backward(u):
        hops(backward, jnp.where(u == step_g, 0, backward_by(u - 1)), backward_by(u))

    def run(start, stop, body):
        def one(u, ignored):
            body(u)
            return ignored

        lax.fori_loop(start, stop, one, 0)

    def opening(u):
        @pl.when(u < step_s)
        def _():
            project(u)

        @pl.when(u >= step_s)
        def _():
            within(u - step_s)

        hops_forward(u)

    def part_first(u):
        b = lax.div(u - step_b, 2)
        hops_forward(u)

        @pl.when(lax.rem(u - step_b, 2) == 0)
        def _():
            over(attend)(b)

        @pl.when(lax.rem(u - step_b, 2) == 1)
        def _():
            feed(0, b)

    def part_between(u):
        @pl.when(u == step_f + blocks)
        def _():
            fill(3)
            filled(2)

        feed(1 + lax.div(u - step_f, blocks), lax.rem(u - step_f, blocks))
        due(u)

    def part_last(u):
        b = lax.div(u - step_g, 2)

        @pl.when(lax.rem(u - step_g, 2) == 0)
        def _():
            feed(3, b)

        @pl.when(lax.rem(u - step_g, 2) == 1)
        def _():
            over(norm_two)(b)
            save(ct, lay_hbm, b).start()

        due(u)
        hops_backward(u)

    def part_query(u):
        query_side(u - step_q)
        due(u)
        hops_backward(u)

    def part_key(u):
        key_side(u - step_k)
        due(u)
        hops_backward(u)

    def closing(u):
        @pl.when(u < step_d)
        def _():
            b = u - step_n
            over(norm_one)(b)
            save(ct, lay_hbm, b).wait()
            save(x, ing_hbm, b).start()

        due(u)
        swaps(u)

    run(0, step_b, opening)
    loads[3].wait()
    filled(0)
    run(step_b, step_f, part_first)
    due(step_f - 1)
    fill(2)
    filled(1)
    run(step_f, step_g, part_between)
    filled(3)
    run(step_g, step_q, part_last)
    run(step_q, step_k, part_query)
    clear(CHUNKS - 1, 0)
    run(step_k, step_n, part_key)
    run(step_n, total_steps, closing)
    sums_ref[...] = sb[...]
    for b in range(blocks):
        save(x, ing_hbm, b).wait()
    for c in range(CHUNKS):
        for copy in results(c)[max(c - 3, 0)][1]:
            copy.wait()


def deliver(scale, sums, *refs):
    big, (peak, hidden), vectors = refs[:8], refs[16:18], refs[18:-9]
    held, sems = refs[-9:-1], refs[-1]
    pieces = []
    for a, b, v in zip(big, refs[8:16], held):
        step = a.shape[0] // 4
        for n in range(4):
            part = pl.ds(n * step, step)
            k = len(pieces)
            pieces.append((pltpu.make_async_copy(a.at[part], v.at[part], sems.at[k, 0]), pltpu.make_async_copy(v.at[part], b.at[part], sems.at[k, 1])))
    for come, _ in pieces:
        come.start()
    peak[0] = jnp.max(sums[PEAK : PEAK + 1, :]) * scale
    hidden[...] = sums[HB : HB + 4, :].reshape(4 * WIDTH)
    for i, ref in enumerate(vectors):
        ref[...] = sums[i : i + 1, :].reshape(WIDTH)
    for come, go in pieces:
        come.wait()
        go.start()
    for _, go in pieces:
        go.wait()


def red_times(steps):
    gaps = [0, 2, 3, 3, 2] + [2] * (steps - 9) + [2, 3, 4, 2]
    total, times = 0, []
    for gap in gaps:
        total += gap
        times.append(total)
    return times


def per_device(
    seq,
    dp,
    tokens,
    short_counts,
    norm1_gain,
    norm1_bias,
    query_weight,
    query_bias,
    key_weight,
    key_bias,
    value_weight,
    value_bias,
    output_weight,
    output_bias,
    norm2_gain,
    norm2_bias,
    hidden_weight,
    hidden_bias,
    return_weight,
    return_bias,
    cotangent,
):
    images, span, width = tokens.shape
    flat = images * span
    per = 2 if images % 2 == 0 else 1
    blocks = images // per
    size = 128 if span % 128 == 0 else span
    dims = [("dp", 1 << k) for k in range(1, dp.bit_length() - 1)]
    dims = dims + [("seq", 1 << k) for k in range(seq.bit_length() - 1)]
    turn = (len(dims) - 1) // 3
    orders = [dims[i * turn :] + dims[: i * turn] for i in range(3)]
    red = Reduce(dims, orders)
    small = (norm1_gain, norm1_bias, query_bias, key_bias, value_bias, output_bias, norm2_gain, norm2_bias, return_bias)
    small = small + (hidden_bias,)
    hbm = pl.BlockSpec(memory_space=pl.ANY)
    vmem = pl.BlockSpec(memory_space=pltpu.VMEM)
    smem = pl.BlockSpec(memory_space=pltpu.SMEM)
    state = (images, 72, QUAD)
    pair = (images, 2, 72, QUAD)
    big = lambda kind: pltpu.VMEM((flat, width), kind)
    f32 = lambda *shape: pltpu.VMEM(shape, F32)
    sem = lambda *shape: pltpu.SemaphoreType.DMA(shape)
    scratch = (
        [big(BF16)] * 8
        + [big(F32)] * 2
        + [pltpu.VMEM((4, width, width), BF16)]
        + [pltpu.VMEM((2, width, PART), BF16), pltpu.VMEM((2, PART, width), BF16)]
        + [f32(LANDS + 4, max(CHUNK, red.rows), width)]
        + [f32(VECS, width)] * 2
        + [f32(len(dims) + 1, VECS, width)]
        + [f32(*pair)]
        + [f32(*state)] * 6
        + [f32(*pair)] * 2
        + [f32(-(-images // 8) * 8, width), f32(images, 8, span), f32(-(-images * (span // size) // 8) * 8, width)]
        + [pltpu.VMEM((4 * size, QUAD), BF16), pltpu.VMEM((QUAD, QUAD), BF16), f32(QUAD, QUAD)]
        + [f32(size, 4 * size)] * 2
        + [sem(2, images), sem(12), sem(blocks), sem(CHUNKS, 2)]
        + [sem(CHUNKS, red.sems)] * 2
        + [pltpu.SemaphoreType.REGULAR((CHUNKS, red.frees))]
        + [sem(images, 3)] * 4
        + [sem(len(dims) + 1)] * 2
    )
    shape = jax.ShapeDtypeStruct
    square = shape((width, width), F32)
    outs = pl.pallas_call(
        functools.partial(kernel, seq, images, span, red, dims),
        out_shape=(
            shape((flat, width), BF16),
            shape((flat, width), BF16),
            shape(return_weight.shape, F32),
            shape(hidden_weight.shape, F32),
            square,
            square,
            square,
            square,
            shape((VECS, width), F32),
        ),
        in_specs=[hbm, hbm, smem, (vmem,) * len(small)] + [hbm] * 6,
        out_specs=(hbm,) * 8 + (vmem,),
        scratch_shapes=scratch,
        compiler_params=pltpu.CompilerParams(
            collective_id=0, has_side_effects=True, vmem_limit_bytes=63 * 2**20
        ),
    )(
        tokens.reshape(flat, width),
        cotangent.reshape(flat, width),
        short_counts,
        small,
        query_weight,
        key_weight,
        value_weight,
        output_weight,
        hidden_weight,
        return_weight,
    )
    results, sums = outs[:8], outs[8]
    smalls = (shape((1,), F32), shape(hidden_bias.shape, F32)) + (shape((width,), F32),) * HB
    outs = pl.pallas_call(
        functools.partial(deliver, 1.0 / (span * seq * (width // HEADS))),
        out_shape=tuple(shape(v.shape, v.dtype) for v in results) + smalls,
        in_specs=[vmem] + [hbm] * 8,
        out_specs=(hbm,) * 8 + (smem,) + (vmem,) * (1 + HB),
        scratch_shapes=[pltpu.VMEM(v.shape, v.dtype) for v in results] + [sem(32, 2)],
        compiler_params=pltpu.CompilerParams(vmem_limit_bytes=63 * 2**20),
    )(sums, *results)
    lay, ing, gw2, gw1, gwo, gwq, gwk, gwv, peak, hidden = outs[:10]
    n1g, n1b, qb, kb, vb, ob, n2g, n2b, rb = outs[10:]
    lay, ing = lay.reshape(tokens.shape), ing.reshape(tokens.shape)
    attention = (gwq, qb, gwk, kb, gwv, vb, gwo, ob)
    return (lay, ing, peak.reshape(()), n1g, n1b) + attention + (n2g, n2b, gw1, hidden, gw2, rb)


def solution(mesh):
    split = P("dp", "seq", None)
    return jax.shard_map(
        functools.partial(per_device, mesh.shape["seq"], mesh.shape["dp"]),
        mesh=mesh,
        in_specs=(split, P("dp")) + (P(),) * 16 + (split,),
        out_specs=(split, split) + (P(),) * 17,
        check_vma=False,
    )
```

time: 286 us -> 228 us (0.80)
  Pallas kernels: 255 us -> 226 us
  local copies, waits for them, and re-layouts: 19.3 us -> 0 us
  other arithmetic: 8.48 us -> 0 us
    pallas_call x1, Pallas kernels: 255 us -> 212 us  [per_device(): pl.pallas_call(functools.partial(kernel, seq, images, span, red, dims), o...]
    unnamed x24 -> x0, local copies, waits for them, and re-layouts: 16.7 us -> none
    pallas_call x0 -> x1, Pallas kernels: none -> 14.1 us  [per_device(): pl.pallas_call(functools.partial(deliver, 1.0 / (span * seq * (width // H...]
    broadcast_in_dim x9 -> x0, other arithmetic: 6.13 us -> none  [per_device(): v.astype(F32)[None]]
where the time goes in v2:
time: 228 us
  Pallas kernels  226 us (99%)
    pallas_call x1, Pallas kernels, per_device(): pl.pallas_call(functools.partial(kernel, seq, images, span, red, dims), o...  212 us
    pallas_call x1, Pallas kernels, per_device(): pl.pallas_call(functools.partial(deliver, 1.0 / (span * seq * (width // H...  14.1 us

profile of v2, /device:TPU:0, one launch (start us, length us, event | category | flops | bytes accessed | tf_op | source)
XLA Modules:
  0.0 227.8 jit_solution(3437392311566054910)
XLA Ops:
  1.3 212.2 %shard_map.330 = (bf16[2304,512]{1,0:T(8,128)(2,1)}, bf16[2304,512]{1,0:T(8,128)(2,1)}, f32[2048,512]{1,0:T(8,128)}, f32[512,2048]{1,0:T(8,128)}, f32[512,512]{1...) custom-call(bf16[2304,512]{1,0:T(8,128)(2,1)} %bitcast.5, ...), custom_call_target="tpu_custom_call" | custom-call | tf_op jit(solution)/shard_map/pallas_call | solution.py:989
  213.5 14.1 %shard_map.331 = (bf16[2304,512]{1,0:T(8,128)(2,1)}, bf16[2304,512]{1,0:T(8,128)(2,1)}, f32[2048,512]{1,0:T(8,128)}, f32[512,2048]{1,0:T(8,128)}, f32[512,512]{1...) custom-call(f32[16,512]{1,0:T(8,128)} %get-tuple-element.47.sums, ...), custom_call_target="tpu_custom_call" | custom-call | tf_op jit(solution)/shard_map/pallas_call | solution.py:1022

commit v3 on v2

--- a/solution.py
+++ b/solution.py
@@ -23,6 +23,7 @@
 CHUNKS = 6
 LANDS = 5
 SHARES = (4, 3, 1)
+LATE_SHARES = (2, 1, 1)
 VECS = 16
 
 
@@ -69,22 +70,27 @@
 
 
 class Reduce:
-    def __init__(self, dims, orders):
+    def __init__(self, dims, orders, rows, shares):
         self.core, self.orders = ("dp", 1), orders
-        self.half = CHUNK // 2
-        unit = self.half // sum(SHARES)
-        self.sizes = [unit * s for s in SHARES]
-        self.starts = [sum(self.sizes[:i]) for i in range(len(SHARES))]
+        self.half = rows // 2
+        unit = self.half // sum(shares)
+        self.sizes = [unit * s for s in shares]
+        self.starts = [sum(self.sizes[:i]) for i in range(len(shares))]
         self.whole = len(dims) - HALVINGS
         self.between = 2 * HALVINGS + self.whole
         self.steps = self.between + 3
-        self.sems = 2 + len(SHARES) * self.between
-        self.frees = 1 + len(SHARES) * (HALVINGS + self.whole)
+        self.sems = 2 + len(shares) * self.between
+        self.dims = [self.core] + dims
+        self.frees = len(self.dims) + len(shares) * self.whole
         self.turn = HALVINGS + self.whole + 1
         self.bases = [self.half]
-        for p in range(len(SHARES)):
+        for p in range(len(shares)):
             self.bases.append(self.bases[-1] + self.offset(p, HALVINGS + self.whole))
         self.rows = self.bases[-1]
+
+    def enter(self):
+        self.bits = {dim: coord(dim) for dim in self.dims}
+        self.peers = {dim: peer(dim) for dim in self.dims}
 
     def offset(self, p, k):
         n = self.sizes[p]
@@ -92,45 +98,45 @@
         return n - (n >> min(k, HALVINGS)) + over * (n >> HALVINGS)
 
     def piece(self, p, k):
-        at = coord(self.core) * self.half + self.starts[p]
+        at = self.bits[self.core] * self.half + self.starts[p]
         for i in range(k):
-            at = at + coord(self.orders[p][i]) * (self.sizes[p] >> (i + 1))
+            at = at + self.bits[self.orders[p][i]] * (self.sizes[p] >> (i + 1))
         return at
 
     def copies(self, g, r, ss, rs, stage):
         half = self.half
         if stage in (0, self.steps - 2):
-            c = coord(self.core)
+            c = self.bits[self.core]
             mine, other = aligned(c * half), aligned((1 - c) * half)
             if stage == 0:
                 dst = r.at[pl.ds(0, half)]
-                cp = remote(g.at[pl.ds(other, half)], dst, ss.at[0], rs.at[0], peer(self.core))
-                return [(cp, mine, 0, half, 0, peer(self.core))]
+                cp = remote(g.at[pl.ds(other, half)], dst, ss.at[0], rs.at[0], self.peers[self.core])
+                return [(cp, mine, 0, half, None, None)]
             part = g.at[pl.ds(mine, half)]
-            cp = remote(part, part, ss.at[1], rs.at[1], peer(self.core))
-            return [(cp, None, None, half, None, peer(self.core))]
+            cp = remote(part, part, ss.at[1], rs.at[1], self.peers[self.core])
+            return [(cp, None, None, half, None, None)]
         out = []
         k = stage - 1
         for p, order in enumerate(self.orders):
             n = self.sizes[p]
             sem = 2 + p * self.between + k
             land = self.bases[p] + self.offset(p, k)
-            free = 1 + p * (HALVINGS + self.whole) + k
+            free = None
             if k < HALVINGS:
                 m, dim, base = n >> (k + 1), order[k], self.piece(p, k)
-                c = coord(dim)
+                c = self.bits[dim]
                 src = g.at[pl.ds(aligned(base + (1 - c) * m), m)]
                 dst, to = r.at[pl.ds(land, m)], aligned(base + c * m)
             elif k < HALVINGS + self.whole:
+                free = len(self.dims) + p * self.whole + k - HALVINGS
                 m, dim, to = n >> HALVINGS, order[k], aligned(self.piece(p, HALVINGS))
                 src, dst = g.at[pl.ds(to, m)], r.at[pl.ds(land, m)]
             else:
                 i = self.between - 1 - k
-                free = None
                 m, dim, to, land = n >> (i + 1), order[i], None, None
                 src = dst = g.at[pl.ds(aligned(self.piece(p, i + 1)), m)]
-            cp = remote(src, dst, ss.at[sem], rs.at[sem], peer(dim))
-            out.append((cp, to, land, m, free, peer(dim)))
+            cp = remote(src, dst, ss.at[sem], rs.at[sem], self.peers[dim])
+            out.append((cp, to, land, m, free, self.peers[dim]))
         return out
 
     def step(self, g, r, ss, rs, fs, k):
@@ -146,21 +152,20 @@
                         return c
 
                     lax.fori_loop(0, m // slab, one, 0)
-                    pl.semaphore_signal(fs.at[free], inc=1, device_id=device, device_id_type=MESH)
-        for n in range(HALVINGS + 1 if k == self.turn else 0):
-            self.freed(fs, n)
-        for n in range(HALVINGS + 1, self.turn if k == self.turn + 1 else 0):
-            self.freed(fs, n)
+                    if free is not None:
+                        pl.semaphore_signal(fs.at[free], inc=1, device_id=device, device_id_type=MESH)
+        if k == HALVINGS + 1:
+            for i, dim in enumerate(self.dims):
+                pl.semaphore_signal(fs.at[i], inc=1, device_id=self.peers[dim], device_id_type=MESH)
+        if k == self.turn:
+            for i in range(len(self.dims)):
+                pl.semaphore_wait(fs.at[i], 1)
+        if k == self.turn + 1:
+            for i in range(len(self.dims), self.frees):
+                pl.semaphore_wait(fs.at[i], 1)
         if k < self.steps - 1:
             for cp, *_ in self.copies(g, r, ss, rs, k):
                 cp.start()
-
-    def freed(self, fs, stage):
-        if stage == 0:
-            pl.semaphore_wait(fs.at[0], 1)
-        else:
-            for p in range(len(SHARES)):
-                pl.semaphore_wait(fs.at[1 + p * (HALVINGS + self.whole) + stage - 1], 1)
 
 
 class Scan:
@@ -286,6 +291,7 @@
     images,
     span,
     red,
+    late,
     dims,
     tok_hbm,
     cot_hbm,
@@ -297,17 +303,10 @@
     wo_hbm,
     w1_hbm,
     w2_hbm,
-    lay_hbm,
-    ing_hbm,
-    gw2_hbm,
-    gw1_hbm,
-    gwo_hbm,
-    gwq_hbm,
-    gwk_hbm,
-    gwv_hbm,
-    sums_ref,
     x,
     ct,
+    g,
+    sums_ref,
     fq,
     fk,
     vb,
@@ -319,7 +318,7 @@
     ws,
     w1,
     w2,
-    g,
+    lands,
     vec,
     sb,
     srx,
@@ -335,6 +334,7 @@
     mu,
     dgt,
     gsum,
+    late_sums,
     mx,
     bo,
     bof,
@@ -342,8 +342,6 @@
     cmt,
     in_sem,
     w_sem,
-    out_sem,
-    go_sem,
     red_ss,
     red_rs,
     red_fs,
@@ -361,6 +359,8 @@
     parts = span // size
     place = lax.axis_index("seq")
     small = [("dp", 1)] + dims
+    red.enter()
+    late.enter()
 
     step_s = images
     step_b = step_s + images
@@ -368,13 +368,22 @@
     step_g = step_f + 2 * blocks
     step_q = step_g + 2 * blocks
     step_k = step_q + images
-    step_n = step_k + images
+    step_n = step_k + 2 * images
     step_d = step_n + blocks
-    times = red_times(red.steps)
-    starts = [step_f - 1, step_f + blocks - 1, step_g - 1, step_q - 2]
-    starts.append(max(step_k - 1, starts[1] + times[red.turn + 1]))
-    starts.append(max(step_n - 1, starts[2] + times[red.turn + 1]))
-    total_steps = max(starts[-1] + times[-1], step_d + len(small)) + 1
+    spans = [13] * step_b + [35, 34] * blocks + [34] * (2 * blocks) + [34, 44] * blocks
+    spans += [23] * images + [16] * (2 * images) + [11] * blocks
+    clock = [sum(spans[: u + 1]) for u in range(len(spans))]
+    clock += [clock[-1] + 20 * n for n in range(1, 80)]
+
+    def places(start, offsets):
+        return [next(u for u, t in enumerate(clock) if t >= clock[start] + d) for d in offsets]
+
+    slow, fast = red_offsets(red, RED_GAPS), red_offsets(late, LATE_GAPS)
+    when = [places(start, slow) for start in (step_f - 1, step_f + blocks - 1, step_g - 1, step_q - 2)]
+    when.append(places(max(step_k - 1, when[1][red.turn + 1]), red_offsets(red, MID_GAPS)))
+    when.append(places(max(step_k + images - 1, when[2][red.turn + 1]), fast))
+    when.append(places(max(step_n - 1, when[2][red.turn + 1]), fast))
+    total_steps = max([step_d + len(small)] + [places_of[-1] for places_of in when]) + 1
 
     def image(i):
         return pl.ds(pl.multiple_of(i * span, 16), span)
@@ -387,9 +396,6 @@
 
     def fetch(hbm, ref, sem, i):
         return pltpu.make_async_copy(hbm.at[image(i)], ref.at[image(i)], sem.at[i])
-
-    def save(ref, hbm, b):
-        return pltpu.make_async_copy(ref.at[block(b)], hbm.at[block(b)], out_sem.at[b])
 
     fetch(tok_hbm, x, in_sem.at[0], 0).start()
     loads = [
@@ -443,6 +449,7 @@
     cm[...] = jnp.where(iota(wide, 1) % size <= iota(wide, 0), 1.0, 0.0)
     cmt[...] = jnp.where(iota(wide, 1) % size >= iota(wide, 0), 1.0, 0.0)
     sb[...] = jnp.zeros_like(sb)
+    late_sums[...] = jnp.zeros_like(late_sums)
 
     def clear(c, ignored):
         def inner(k, ignored):
@@ -617,13 +624,16 @@
         totals = den_grad * query.astype(F32)
         totals = [colsum(totals[c * size : (c + 1) * size]) for c in range(parts)]
         for c in range(1, parts):
-            gsum[pl.ds(i * parts + c, 1), :] = totals[c]
+            for q, cols in enumerate(halves):
+                gsum[i * parts + c, q, 0:1, :] = totals[c][:, cols]
         total = functools.reduce(lambda a, b: a + b, totals)
         for q, cols in enumerate(halves):
             put(i, q, tn(query[:, cols], num_grad[:, cols]) * bof[...], total[:, cols])
         backward.begin(i)
         pick = jnp.where(iota((8, WIDTH), 1) == iota((8, WIDTH), 0) * DEPTH, 1.0, 0.0).astype(BF16)
-        dgt[i] = nt(pick, high) + nt(pick, low_part)
+        line = nt(pick, high) + nt(pick, low_part)
+        dgt[i, 0, 0:4, :] = line[0:4]
+        dgt[i, 1, 0:4, :] = line[4:8]
         g[4, 0:512, :] += tn(attn, low)
         add(OB, colsum(low.astype(F32)))
 
@@ -653,42 +663,40 @@
     def spread_rows(v):
         return [u[:, :size] for u in spread(v)]
 
-    def key_side(i):
-        backward.end(i)
+    def key_side(i, q):
+        cols = pl.ds(pl.multiple_of(q * QUAD, QUAD), QUAD)
         first = at[image(i), :]
+        state, total = known(b_prior, i, q)
+        states, totals = [], []
+        for c in reversed(range(parts)):
+            states.insert(0, split(state))
+            totals.insert(0, total)
+            if c > 0:
+                state = state + tn(fq[spot(i, c), cols], si[spot(i, c), cols]) * bof[...]
+                total = total + gsum[i * parts + c, q, 0:1, :]
+        wide_query = [four(fq[spot(i, c), cols]) * mx[...] for c in range(parts)]
+        wide_num = [four(si[spot(i, c), cols]) * mx[...] for c in range(parts)]
+        key = [fk[spot(i, c), cols] for c in range(parts)]
+        value = [vb[spot(i, c), cols] for c in range(parts)]
+        score = [(nt(k, u) * cmt[...]).astype(BF16) for k, u in zip(key, wide_query)]
+        value_part = [mm(v, u) for v, u in zip(score, wide_num)]
+        back = []
+        for c in range(parts):
+            line = [dgt[i, q, h : h + 1, c * size : (c + 1) * size] for h in range(4)]
+            line = jnp.concatenate(line, axis=1)
+            back.append(((nt(value[c], wide_num[c]) + line) * cmt[...]).astype(BF16))
+        key_part = [mm(v, u) for v, u in zip(back, wide_query)]
         low_k, low_v = [], []
-        for q in range(2):
-            state, total = known(b_prior, i, q)
-            states, totals = [], []
-            for c in reversed(range(parts)):
-                states.insert(0, split(state))
-                totals.insert(0, total)
-                if c > 0:
-                    state = state + tn(read(fq, i, q, c), read(si, i, q, c)) * bof[...]
-                    total = total + gsum[pl.ds(i * parts + c, 1), halves[q]]
-            wide_query = [four(read(fq, i, q, c)) * mx[...] for c in range(parts)]
-            wide_num = [four(read(si, i, q, c)) * mx[...] for c in range(parts)]
-            key = [read(fk, i, q, c) for c in range(parts)]
-            value = [read(vb, i, q, c) for c in range(parts)]
-            score = [(nt(k, u) * cmt[...]).astype(BF16) for k, u in zip(key, wide_query)]
-            value_part = [mm(v, u) for v, u in zip(score, wide_num)]
-            back = []
-            for c in range(parts):
-                line = [dgt[i, 4 * q + h : 4 * q + h + 1, c * size : (c + 1) * size] for h in range(4)]
-                line = jnp.concatenate(line, axis=1)
-                back.append(((nt(value[c], wide_num[c]) + line) * cmt[...]).astype(BF16))
-            key_part = [mm(v, u) for v, u in zip(back, wide_query)]
-            for c in range(parts):
-                (high, part), total = states[c], totals[c]
-                grad = key_part[c] + nt(value[c], high) + nt(value[c], part) + total
-                low_k.append((grad * jnp.minimum(key[c].astype(F32), 1.0)).astype(BF16))
-                low_v.append((value_part[c] + mm(key[c], high)).astype(BF16))
-        low_k, low_v = together(low_k), together(low_v)
-        g[5, 0:512, :] += tn(first, low_k)
-        g[5, 512:1024, :] += tn(first, low_v)
-        add(KB, colsum(low_k.astype(F32)))
-        add(VB, colsum(low_v.astype(F32)))
-        out[image(i), :] += nt(low_k, ws[1]) + nt(low_v, ws[2])
+        for c in range(parts):
+            (high, part), total = states[c], totals[c]
+            grad = key_part[c] + nt(value[c], high) + nt(value[c], part) + total
+            low_k.append((grad * jnp.minimum(key[c].astype(F32), 1.0)).astype(BF16))
+            low_v.append((value_part[c] + mm(key[c], high)).astype(BF16))
+        low_k, low_v = jnp.concatenate(low_k, axis=0), jnp.concatenate(low_v, axis=0)
+        both = jnp.concatenate([low_k, low_v], axis=1)
+        g[5, pl.ds(pl.multiple_of(q * 512, 512), 512), :] += tn(first, both)
+        late_sums[q, 0:1, :] += colsum(both.astype(F32))
+        out[image(i), :] += nt(low_k, ws[1, :, cols]) + nt(low_v, ws[2, :, cols])
 
     def norm_one(i):
         part = image(i)
@@ -708,36 +716,27 @@
 
         return run
 
-    def results(c):
-        cols = pl.ds(pl.multiple_of(c * PART, PART), PART)
-        two = [
-            (c < 4, gw2_hbm.at[cols, :], gw1_hbm.at[:, cols]),
-            (c == 4, gwo_hbm, gwq_hbm),
-            (c == 5, gwk_hbm, gwv_hbm),
-        ]
-        upper, lower = g.at[c, pl.ds(0, 512)], g.at[c, pl.ds(512, 512)]
-        return [
-            (when, (pltpu.make_async_copy(upper, a, go_sem.at[c, 0]), pltpu.make_async_copy(lower, b, go_sem.at[c, 1])))
-            for when, a, b in two
-        ]
-
-    def due(u):
-        for k in reversed(range(red.steps)):
-            c = -1
-            for n, start in enumerate(starts):
-                c = jnp.where(u == start + times[k], n, c)
-
-            @pl.when(c >= 0)
-            def _(k=k, c=c):
-                land = LANDS + c - jnp.where(c >= 4, 3, 0)
-                red.step(g.at[c], g.at[land], red_ss.at[c], red_rs.at[c], red_fs.at[c], k)
-                if k == red.steps - 1:
-                    for when, copies in results(c):
-
-                        @pl.when(when)
-                        def _(copies=copies):
-                            for copy in copies:
-                                copy.start()
+    events = sorted((u, c, k) for c, line in enumerate(when) for k, u in enumerate(line))
+
+    def advance(c, k):
+        sems = (red_ss.at[c], red_rs.at[c], red_fs.at[c])
+        if c < 5:
+            land = g.at[CHUNKS - 1] if c == 0 else lands.at[c - 1 if c < 4 else 0]
+            red.step(g.at[c], land, *sems, k)
+        else:
+            mine = g.at[5, pl.ds((c - 5) * 512, 512)]
+            late.step(mine, lands.at[1, pl.ds((c - 5) * late.rows, late.rows)], *sems, k)
+
+    def due(u, start, stop):
+        for at_step, c, k in events:
+            if isinstance(u, int):
+                if at_step == u:
+                    advance(c, k)
+            elif start <= at_step < stop:
+
+                @pl.when(u == at_step)
+                def _(c=c, k=k):
+                    advance(c, k)
 
     def swap(k):
         return remote(sb, srx.at[k], s_ss.at[k], s_rs.at[k], peer(small[k]))
@@ -746,8 +745,7 @@
         peaks = iota((VECS, WIDTH), 0) == PEAK
         for k in range(len(small) + 1):
 
-            @pl.when(u == step_d + k)
-            def _(k=k):
+            if u == step_d + k:
                 if k > 0:
                     swap(k - 1).wait()
                     came = srx[k - 1]
@@ -785,7 +783,7 @@
     def backward_by(u):
         v, w, y = u - step_g, u - step_q, u - step_k
         in_g = 78 * lax.div(v, 2) + jnp.where(lax.rem(v, 2) == 0, 34, 78)
-        now = jnp.where(u < step_q, in_g, jnp.where(u < step_k, 78 * blocks + 24 * (w + 1), 78 * blocks + 24 * images + 33 * (y + 1)))
+        now = jnp.where(u < step_q, in_g, jnp.where(u < step_k, 78 * blocks + 24 * (w + 1), 78 * blocks + 24 * images + 17 * (y + 1)))
         least = jnp.clip(jnp.where(u < step_k - 1, 0, y + 2), 0, images)
         return ready(backward, turned, now - 20, least)
 
@@ -829,7 +827,7 @@
             filled(2)
 
         feed(1 + lax.div(u - step_f, blocks), lax.rem(u - step_f, blocks))
-        due(u)
+        due(u, step_f, step_g)
 
     def part_last(u):
         b = lax.div(u - step_g, 2)
@@ -841,37 +839,38 @@
         @pl.when(lax.rem(u - step_g, 2) == 1)
         def _():
             over(norm_two)(b)
-            save(ct, lay_hbm, b).start()
-
-        due(u)
+
+        due(u, step_g, step_q)
         hops_backward(u)
 
     def part_query(u):
         query_side(u - step_q)
-        due(u)
+        due(u, step_q, step_k)
         hops_backward(u)
 
     def part_key(u):
-        key_side(u - step_k)
-        due(u)
+        i, q = lax.rem(u - step_k, images), lax.div(u - step_k, images)
+
+        @pl.when(q == 0)
+        def _():
+            backward.end(i)
+
+        key_side(i, q)
+        due(u, step_k, step_n)
         hops_backward(u)
 
     def closing(u):
-        @pl.when(u < step_d)
-        def _():
+        if u < step_d:
             b = u - step_n
             over(norm_one)(b)
-            save(ct, lay_hbm, b).wait()
-            save(x, ing_hbm, b).start()
-
-        due(u)
+        due(u, u, u + 1)
         swaps(u)
 
     run(0, step_b, opening)
     loads[3].wait()
     filled(0)
     run(step_b, step_f, part_first)
-    due(step_f - 1)
+    due(step_f - 1, 0, 0)
     fill(2)
     filled(1)
     run(step_f, step_g, part_between)
@@ -880,45 +879,47 @@
     run(step_q, step_k, part_query)
     clear(CHUNKS - 1, 0)
     run(step_k, step_n, part_key)
-    run(step_n, total_steps, closing)
+    for q, cols in enumerate(halves):
+        sb[KB : KB + 1, cols] = late_sums[q, 0:1, 0:QUAD]
+        sb[VB : VB + 1, cols] = late_sums[q, 0:1, QUAD:WIDTH]
+    for u in range(step_n, total_steps):
+        closing(u)
     sums_ref[...] = sb[...]
-    for b in range(blocks):
-        save(x, ing_hbm, b).wait()
-    for c in range(CHUNKS):
-        for copy in results(c)[max(c - 3, 0)][1]:
-            copy.wait()
-
-
-def deliver(scale, sums, *refs):
-    big, (peak, hidden), vectors = refs[:8], refs[16:18], refs[18:-9]
-    held, sems = refs[-9:-1], refs[-1]
-    pieces = []
-    for a, b, v in zip(big, refs[8:16], held):
-        step = a.shape[0] // 4
-        for n in range(4):
-            part = pl.ds(n * step, step)
-            k = len(pieces)
-            pieces.append((pltpu.make_async_copy(a.at[part], v.at[part], sems.at[k, 0]), pltpu.make_async_copy(v.at[part], b.at[part], sems.at[k, 1])))
-    for come, _ in pieces:
-        come.start()
+
+
+def deliver(scale, ing, lay, g, sums, *refs):
+    ing_out, lay_out, gw2, gw1, gwo, gwq, gwk, gwv, peak, hidden = refs[:10]
+    sems = refs[-1]
+    pairs = [(ing, ing_out), (lay, lay_out)]
+    for c in range(4):
+        cols = pl.ds(c * PART, PART)
+        pairs += [(g.at[c, pl.ds(0, 512)], gw2.at[cols, :]), (g.at[c, pl.ds(512, 512)], gw1.at[:, cols])]
+    pairs += [(g.at[4, pl.ds(0, 512)], gwo), (g.at[4, pl.ds(512, 512)], gwq)]
+    for q in range(2):
+        rows, cols = pl.ds(q * 512, 512), pl.ds(q * QUAD, QUAD)
+        pairs += [
+            (g.at[5, rows, pl.ds(0, QUAD)], gwk.at[:, cols]),
+            (g.at[5, rows, pl.ds(QUAD, QUAD)], gwv.at[:, cols]),
+        ]
+    copies = [pltpu.make_async_copy(a, b, sems.at[i]) for i, (a, b) in enumerate(pairs)]
+    for copy in copies:
+        copy.start()
     peak[0] = jnp.max(sums[PEAK : PEAK + 1, :]) * scale
     hidden[...] = sums[HB : HB + 4, :].reshape(4 * WIDTH)
-    for i, ref in enumerate(vectors):
+    for i, ref in enumerate(refs[10:-1]):
         ref[...] = sums[i : i + 1, :].reshape(WIDTH)
-    for come, go in pieces:
-        come.wait()
-        go.start()
-    for _, go in pieces:
-        go.wait()
-
-
-def red_times(steps):
-    gaps = [0, 2, 3, 3, 2] + [2] * (steps - 9) + [2, 3, 4, 2]
-    total, times = 0, []
-    for gap in gaps:
-        total += gap
-        times.append(total)
-    return times
+    for copy in copies:
+        copy.wait()
+
+
+RED_GAPS = (40, 100, 80, 60, 50, 50, 70, 100, 50)
+MID_GAPS = (35, 80, 55, 45, 40, 40, 50, 80, 40)
+LATE_GAPS = (30, 55, 40, 32, 32, 32, 40, 55, 30)
+
+
+def red_offsets(red, gaps):
+    gaps = gaps[:4] + gaps[4:5] * (red.steps - 9) + gaps[5:] if red.steps > 9 else gaps[: red.steps - 1]
+    return [sum(gaps[:k]) for k in range(red.steps)]
 
 
 def per_device(
@@ -953,7 +954,8 @@
     dims = dims + [("seq", 1 << k) for k in range(seq.bit_length() - 1)]
     turn = (len(dims) - 1) // 3
     orders = [dims[i * turn :] + dims[: i * turn] for i in range(3)]
-    red = Reduce(dims, orders)
+    red = Reduce(dims, orders, CHUNK, SHARES)
+    late = Reduce(dims, orders, CHUNK // 2, LATE_SHARES)
     small = (norm1_gain, norm1_bias, query_bias, key_bias, value_bias, output_bias, norm2_gain, norm2_bias, return_bias)
     small = small + (hidden_bias,)
     hbm = pl.BlockSpec(memory_space=pl.ANY)
@@ -965,45 +967,41 @@
     f32 = lambda *shape: pltpu.VMEM(shape, F32)
     sem = lambda *shape: pltpu.SemaphoreType.DMA(shape)
     scratch = (
-        [big(BF16)] * 8
+        [big(BF16)] * 6
         + [big(F32)] * 2
         + [pltpu.VMEM((4, width, width), BF16)]
         + [pltpu.VMEM((2, width, PART), BF16), pltpu.VMEM((2, PART, width), BF16)]
-        + [f32(LANDS + 4, max(CHUNK, red.rows), width)]
+        + [f32(3, max(CHUNK, red.rows, 2 * late.rows), width)]
         + [f32(VECS, width)] * 2
         + [f32(len(dims) + 1, VECS, width)]
         + [f32(*pair)]
         + [f32(*state)] * 6
         + [f32(*pair)] * 2
-        + [f32(-(-images // 8) * 8, width), f32(images, 8, span), f32(-(-images * (span // size) // 8) * 8, width)]
+        + [f32(-(-images // 8) * 8, width), f32(images, 2, 8, span), f32(images * (span // size), 2, 8, QUAD)]
+        + [f32(2, 8, width)]
         + [pltpu.VMEM((4 * size, QUAD), BF16), pltpu.VMEM((QUAD, QUAD), BF16), f32(QUAD, QUAD)]
         + [f32(size, 4 * size)] * 2
-        + [sem(2, images), sem(12), sem(blocks), sem(CHUNKS, 2)]
-        + [sem(CHUNKS, red.sems)] * 2
-        + [pltpu.SemaphoreType.REGULAR((CHUNKS, red.frees))]
+        + [sem(2, images), sem(12)]
+        + [sem(CHUNKS + 1, red.sems)] * 2
+        + [pltpu.SemaphoreType.REGULAR((CHUNKS + 1, red.frees))]
         + [sem(images, 3)] * 4
         + [sem(len(dims) + 1)] * 2
     )
     shape = jax.ShapeDtypeStruct
     square = shape((width, width), F32)
     outs = pl.pallas_call(
-        functools.partial(kernel, seq, images, span, red, dims),
+        functools.partial(kernel, seq, images, span, red, late, dims),
         out_shape=(
-            shape((flat, width), BF16),
-            shape((flat, width), BF16),
-            shape(return_weight.shape, F32),
-            shape(hidden_weight.shape, F32),
-            square,
-            square,
-            square,
-            square,
-            shape((VECS, width), F32),
+            big(BF16),
+            big(BF16),
+            f32(CHUNKS, max(CHUNK, red.rows), width),
+            f32(VECS, width),
         ),
         in_specs=[hbm, hbm, smem, (vmem,) * len(small)] + [hbm] * 6,
-        out_specs=(hbm,) * 8 + (vmem,),
+        out_specs=(vmem,) * 4,
         scratch_shapes=scratch,
         compiler_params=pltpu.CompilerParams(
-            collective_id=0, has_side_effects=True, vmem_limit_bytes=63 * 2**20
+            collective_id=0, has_side_effects=True, vmem_limit_bytes=46 * 2**20
         ),
     )(
         tokens.reshape(flat, width),
@@ -1017,17 +1015,18 @@
         hidden_weight,
         return_weight,
     )
-    results, sums = outs[:8], outs[8]
+    rowed = shape((flat, width), BF16)
     smalls = (shape((1,), F32), shape(hidden_bias.shape, F32)) + (shape((width,), F32),) * HB
+    bigs = (rowed, rowed, shape(return_weight.shape, F32), shape(hidden_weight.shape, F32)) + (square,) * 4
     outs = pl.pallas_call(
         functools.partial(deliver, 1.0 / (span * seq * (width // HEADS))),
-        out_shape=tuple(shape(v.shape, v.dtype) for v in results) + smalls,
-        in_specs=[vmem] + [hbm] * 8,
+        out_shape=bigs + smalls,
+        in_specs=[vmem] * 4,
         out_specs=(hbm,) * 8 + (smem,) + (vmem,) * (1 + HB),
-        scratch_shapes=[pltpu.VMEM(v.shape, v.dtype) for v in results] + [sem(32, 2)],
-        compiler_params=pltpu.CompilerParams(vmem_limit_bytes=63 * 2**20),
-    )(sums, *results)
-    lay, ing, gw2, gw1, gwo, gwq, gwk, gwv, peak, hidden = outs[:10]
+        scratch_shapes=[sem(16)],
+        compiler_params=pltpu.CompilerParams(vmem_limit_bytes=4 * 2**20),
+    )(*outs)
+    ing, lay, gw2, gw1, gwo, gwq, gwk, gwv, peak, hidden = outs[:10]
     n1g, n1b, qb, kb, vb, ob, n2g, n2b, rb = outs[10:]
     lay, ing = lay.reshape(tokens.shape), ing.reshape(tokens.shape)
     attention = (gwq, qb, gwk, kb, gwv, vb, gwo, ob)

time: 228 us -> 219 us (0.961)
  Pallas kernels: 226 us -> 217 us
    pallas_call x1, Pallas kernels: 14.1 us -> 6.77 us  [per_device(): pl.pallas_call(functools.partial(deliver, 1.0 / (span * seq * (width // H...]
where the time goes in v3:
time: 219 us
  Pallas kernels  217 us (99%)
    pallas_call x1, Pallas kernels, per_device(): pl.pallas_call(functools.partial(kernel, seq, images, span, red, late, di...  211 us
    pallas_call x1, Pallas kernels, per_device(): pl.pallas_call(functools.partial(deliver, 1.0 / (span * seq * (width // H...  6.77 us

profile of v3, /device:TPU:0, one launch (start us, length us, event | category | flops | bytes accessed | tf_op | source)
XLA Modules:
  0.0 218.8 jit_solution(16341450251925187284)
XLA Ops:
  1.3 210.6 %shard_map.330 = (bf16[2304,512]{1,0:T(8,128)(2,1)S(1)}, bf16[2304,512]{1,0:T(8,128)(2,1)S(1)}, f32[6,1024,512]{2,1,0:T(8,128)S(1)}, f32[16,512]{1,0:T(8,128)S(1)}) custom-call(bf16[2304,512]{1,0:T(8,128)(2,1)} %bitcast.5, bf16[2304,512]{1,0:T(8,128)(2,1)} %bitcast.6, s32[1]{0:T(128)S(6)} %copy.38.short_ref, bf16[512]{0:T(512)(128)(2,1)} %vec_refs_0_.1, ...), custom_call_target="tpu_custom_call" | custom-call | tf_op jit(solution)/shard_map/pallas_call | solution.py:992
  211.9 6.8 %shard_map.331 = (bf16[2304,512]{1,0:T(8,128)(2,1)}, bf16[2304,512]{1,0:T(8,128)(2,1)}, f32[2048,512]{1,0:T(8,128)}, f32[512,2048]{1,0:T(8,128)}, f32[512,512]{1...) custom-call(bf16[2304,512]{1,0:T(8,128)(2,1)S(1)} %get-tuple-element, ...), custom_call_target="tpu_custom_call" | custom-call | tf_op jit(solution)/shard_map/pallas_call | solution.py:1021

commit v4 on v3

--- a/solution.py
+++ b/solution.py
@@ -253,9 +253,8 @@
 def normal_parts(u):
     e = jnp.exp(-0.5 * u * u)
     t = 1.0 / (1.0 + 0.3275911 * 0.7071067811865476 * jnp.abs(u))
-    poly = 1.421413741 + t * (-1.453152027 + t * 1.061405429)
-    poly = t * (0.254829592 + t * (-0.284496736 + t * poly))
-    tail = 0.5 * poly * e
+    poly = 0.7107068705 + t * (-0.7265760135 + t * 0.5307027145)
+    tail = t * (0.127414796 + t * (-0.142248368 + t * poly)) * e
     return jnp.where(u > 0, 1.0 - tail, tail), e * 0.3989422804014327
 
 
@@ -716,7 +715,8 @@
 
         return run
 
-    events = sorted((u, c, k) for c, line in enumerate(when) for k, u in enumerate(line))
+    events = [(u, c, k) for c, line in enumerate(when) for k, u in enumerate(line)]
+    events.sort(key=lambda e: (e[0], e[1] if e[0] < step_n else -e[1]))
 
     def advance(c, k):
         sems = (red_ss.at[c], red_rs.at[c], red_fs.at[c])
@@ -912,7 +912,7 @@
         copy.wait()
 
 
-RED_GAPS = (40, 100, 80, 60, 50, 50, 70, 100, 50)
+RED_GAPS = (52, 130, 104, 78, 65, 65, 91, 130, 65)
 MID_GAPS = (35, 80, 55, 45, 40, 40, 50, 80, 40)
 LATE_GAPS = (30, 55, 40, 32, 32, 32, 40, 55, 30)
 

time: 219 us -> 216 us (0.986)
  Pallas kernels: 217 us -> 214 us
    pallas_call x1, Pallas kernels: 211 us -> 208 us  [per_device(): pl.pallas_call(functools.partial(kernel, seq, images, span, red, late, di...]
where the time goes in v4:
time: 216 us
  Pallas kernels  214 us (99%)
    pallas_call x1, Pallas kernels, per_device(): pl.pallas_call(functools.partial(kernel, seq, images, span, red, late, di...  208 us
    pallas_call x1, Pallas kernels, per_device(): pl.pallas_call(functools.partial(deliver, 1.0 / (span * seq * (width // H...  6.77 us

profile of v4, /device:TPU:0, one launch (start us, length us, event | category | flops | bytes accessed | tf_op | source)
XLA Modules:
  0.0 215.8 jit_solution(3121238840351055717)
XLA Ops:
  1.3 207.5 %shard_map.330 = (bf16[2304,512]{1,0:T(8,128)(2,1)S(1)}, bf16[2304,512]{1,0:T(8,128)(2,1)S(1)}, f32[6,1024,512]{2,1,0:T(8,128)S(1)}, f32[16,512]{1,0:T(8,128)S(1)}) custom-call(bf16[2304,512]{1,0:T(8,128)(2,1)} %bitcast.5, bf16[2304,512]{1,0:T(8,128)(2,1)} %bitcast.6, s32[1]{0:T(128)S(6)} %copy.38.short_ref, bf16[512]{0:T(512)(128)(2,1)} %vec_refs_0_.1, ...), custom_call_target="tpu_custom_call" | custom-call | tf_op jit(solution)/shard_map/pallas_call | solution.py:992
  208.8 6.8 %shard_map.331 = (bf16[2304,512]{1,0:T(8,128)(2,1)}, bf16[2304,512]{1,0:T(8,128)(2,1)}, f32[2048,512]{1,0:T(8,128)}, f32[512,2048]{1,0:T(8,128)}, f32[512,512]{1...) custom-call(bf16[2304,512]{1,0:T(8,128)(2,1)S(1)} %get-tuple-element, ...), custom_call_target="tpu_custom_call" | custom-call | tf_op jit(solution)/shard_map/pallas_call | solution.py:1021
